TPU v7x, 128 devices: a whole 4x4x4 slice. The times are simulated.
128 devices in a mesh: row: 32 (over y, z, core), col: 4 (over x).
Axes of the slice: x: 4, y: 4, z: 4, core: 2. Of those that a mesh axis runs over, the one named last changes fastest.
Arguments:
- adjoint: float32 [32, 32, 8, 8, 4, 256], P(None, 'row', None, None, 'col'), may hold values from -6 to 6
- lower_panels: float32 [2, 8, 4, 32, 8, 256], P(None, None, 'col', 'row'), may hold values from -0.16 to 2, as said below
- diag_inverse: float32 [2, 256, 256], replicated, may hold values from -0.16 to 1.5, as said below
Outputs:
- symmetric_adjoint: float32 [32, 32, 8, 8, 4, 256], P(None, 'row', None, None, 'col')
Inputs may be any that keep to these rules, and one draw needn't show every extreme that they name: `lower_panels`: row blocks of panel k before block k are zero; its block k is lower triangular with diagonal entries between 1 and 2. `diag_inverse`: each matrix is lower triangular with diagonal entries between 0.5 and 1.5.
All inputs are finite; a program needn't handle non-finite values.
Results may differ from a plain program's by a relative error of at most 0.00011.
Values sent between devices are 32-bit elements; how exact they have to be, the bound alone decides.
No kernel may reach another device: no remote copies, remote signals or barrier semaphores. Data moves between devices by JAX's collectives and lax.ppermute only.
A program may use at most 192 MiB of HBM per device.

v0:
```python
import jax
import jax.numpy as jnp
from jax import lax
from jax.experimental import pallas as pl
from jax.experimental.pallas import tpu as pltpu
from jax.sharding import PartitionSpec as P

BLK = 256
RSUB = 8
LOC_C = 8
N_ROW = 32
N_COL = 4
NBLK = 32
ROWS = NBLK * RSUB
COLS = LOC_C * BLK
LINES = ROWS * COLS // 128
STRIP = LOC_C * RSUB
PIECE = 2 * STRIP
N_CHIP = 16
RING = (0, 1, 3, 2)
F32 = jnp.float32
BF16 = jnp.bfloat16
VMEM_LIMIT = 56 * 1024 * 1024
SMALL_LIMIT = 24 * 1024 * 1024
SMEM = pl.BlockSpec(memory_space=pltpu.SMEM)


def shape(*dims, dtype=F32):
    return jax.ShapeDtypeStruct(dims, dtype)


def call(
    body, outs, ins, scratch=(), heads=None, raw_in=(), raw_out=(), near=(), aliases=None, eager=True,
    flops=0, size=0,
):
    count, results = len(ins), len(outs)
    heads = heads or {}
    staged_in = [i for i in range(count) if i not in raw_in and i not in near]
    staged_out = [i for i in range(results) if i not in raw_out]

    def kernel(*refs):
        refs = list(refs)
        place = refs.pop(0)
        sources, refs = refs[:count], refs[count:]
        targets, refs = refs[:results], refs[results:]
        staged, made = list(sources), list(targets)
        for i in staged_in:
            staged[i] = refs.pop(0)
        for i in staged_out:
            made[i] = refs.pop(0)
        in_sem, out_sem = refs[-2:]
        copies = {
            i: pltpu.make_async_copy(
                sources[i].at[pl.ds(0, heads[i])] if i in heads else sources[i],
                staged[i],
                in_sem.at[i],
            )
            for i in staged_in
        }
        leaving = {
            i: pltpu.make_async_copy(made[i], targets[i], out_sem.at[i]) for i in staged_out
        }

        def begin():
            for copy in copies.values():
                copy.start()

        if eager:
            begin()
        body(
            place,
            staged,
            lambda *which: begin()
            if which == (None,)
            else [copies[i].wait() for i in which if i in copies],
            made,
            lambda *which: [leaving[i].start() for i in which],
            *refs[:-2],
        )
        for copy in leaving.values():
            copy.wait()

    anywhere = pl.BlockSpec(memory_space=pl.ANY)
    nearby = pl.BlockSpec(memory_space=pltpu.VMEM)
    return pl.pallas_call(
        kernel,
        out_shape=list(outs),
        in_specs=[SMEM] + [nearby if i in near else anywhere for i in range(count)],
        out_specs=[anywhere] * results,
        scratch_shapes=[
            pltpu.VMEM((heads.get(i, ins[i].shape[0]), *ins[i].shape[1:]), ins[i].dtype)
            for i in staged_in
        ]
        + [pltpu.VMEM(outs[i].shape, outs[i].dtype) for i in staged_out]
        + list(scratch)
        + [pltpu.SemaphoreType.DMA((count,)), pltpu.SemaphoreType.DMA((results,))],
        input_output_aliases=aliases or {},
        compiler_params=pltpu.CompilerParams(vmem_limit_bytes=SMALL_LIMIT if near else VMEM_LIMIT),
        cost_estimate=pl.CostEstimate(flops=flops, bytes_accessed=size, transcendentals=0),
    )


def split(value):
    high = value.astype(BF16)
    return high, (value - high.astype(F32)).astype(BF16)


def dot_split(left, right):
    left_high, left_low = left
    right_high, right_low = right
    return jnp.dot(
        jnp.concatenate([left_high, left_high, left_low], axis=1),
        jnp.concatenate([right_high, right_low, right_high], axis=0),
        preferred_element_type=F32,
    )


def beside(left, right):
    return tuple(jnp.concatenate(pair, axis=1) for pair in zip(left, right))


def dot3(left, right):
    return dot_split(split(left), split(right))


def dot3t(left, right):
    return dot3(left.T, right)


def swap_groups(tiles):
    tiles = list(tiles)
    group = lax.broadcasted_iota(jnp.int32, (8, 128), 1) // 8
    for bit in (1, 2, 4, 8):
        keep = (group & bit) == 0
        for i in range(16):
            if i & bit:
                continue
            a, b = tiles[i], tiles[i | bit]
            tiles[i] = jnp.where(keep, a, pltpu.roll(b, 8 * bit, 1))
            tiles[i | bit] = jnp.where(keep, pltpu.roll(a, 128 - 8 * bit, 1), b)
    return tiles


def pack_body(
    place_ref, staged, wait, made, flush, lines_ref, turned_ref, packed_ref, in_sem, out_sem
):
    (source_ref,), (out_ref, matrix_ref) = staged, made
    arriving = [
        pltpu.make_async_copy(source_ref.at[high], lines_ref.at[high], in_sem.at[high])
        for high in range(2)
    ]
    for copy in arriving:
        copy.start()
    for high in range(2):
        arriving[high].wait()

        def first(group, carry):
            for half in range(2):
                tiles = []
                for col in range(N_COL):
                    for low in range(4):
                        start = (4 * low + col) * 128 + group * 2 + half
                        tile = lines_ref[high, pl.ds(start, 8, stride=16), :]
                        block = 16 * high + 4 * low + col
                        matrix_ref[group, block * 8 : block * 8 + 8, half * 128 : half * 128 + 128] = tile
                        tiles.append(tile)
                turned = jnp.concatenate(tiles, axis=0).T
                turned_ref[high, group, half * 128 : half * 128 + 128, :] = turned
            return carry

        lax.fori_loop(0, LOC_C, first, 0, unroll=2)
    flush(1)
    leaving = []
    for part in range(4):

        def second(index, carry):
            row = part * 8 + index
            tiles = [
                turned_ref[high, group, pl.ds(row * 8, 8), :]
                for high in range(2)
                for group in range(LOC_C)
            ]
            packed_ref[part, pl.ds(index * 128, 128), :] = jnp.concatenate(tiles, axis=0).T
            return carry

        lax.fori_loop(0, 8, second, 0, unroll=4)
        leaving.append(
            pltpu.make_async_copy(packed_ref.at[part], out_ref.at[part], out_sem.at[part])
        )
        leaving[part].start()
    for copy in leaving:
        copy.wait()


def mirror_tiles(piece_ref, low, half):
    tiles = [piece_ref[half * 16 + sub, pl.ds(low * 8, 8), :] for sub in range(16)]
    turned = jnp.concatenate(tiles, axis=0).T
    return {
        (high, group): turned[high * 64 + group * 8 : high * 64 + group * 8 + 8]
        for high in range(2)
        for group in range(LOC_C)
    }


def half_kernel(lines_ref, arrived_ref, out_ref):
    def turn(low, carry):
        for half in range(2):
            for (high, group), tile in mirror_tiles(arrived_ref.at[:, 0], low, half).items():
                rows = pl.ds((4 * high + low) * 2 + half, 8, stride=16)
                out_ref[group, 0, rows, :] = 0.5 * (lines_ref[group, 0, rows, :] + tile)
        return carry

    lax.fori_loop(0, 4, turn, 0, unroll=2)


def half_sum(lines, arrived):
    split_lines = (LOC_C, N_COL, 128, 128)
    block = pl.BlockSpec((LOC_C, 1, 128, 128), lambda i: (0, i, 0, 0))
    return pl.pallas_call(
        half_kernel,
        grid=(N_COL,),
        out_shape=shape(*split_lines),
        in_specs=[block, pl.BlockSpec((N_ROW, 1, 32, 128), lambda i: (0, i, 0, 0))],
        out_specs=block,
        compiler_params=pltpu.CompilerParams(vmem_limit_bytes=VMEM_LIMIT),
        cost_estimate=pl.CostEstimate(flops=0, bytes_accessed=2**24, transcendentals=0),
    )(lines.reshape(split_lines), arrived)


def direct_body(
    place_ref, staged, wait, made, flush, one_ref, zero_ref, left_ref, image_ref, square_ref, heads_ref
):
    matrix_ref, *pieces = staged[:9]
    inverse_ref = staged[9]
    panels = staged[10:14]
    leads = staged[14:16]
    rest_ref, high_ref, low_ref, keep_ref, give_ref = made
    row_y, row_z, core, col_place = (place_ref[i] for i in range(1, 5))
    is_zero = col_place == 0
    is_one = col_place == 1
    mine = pl.ds(pl.multiple_of(place_ref[0] * 8, 8), 8)
    wait(*range(1, 9))
    for side in range(2):
        moved = core if side == 0 else 1 - core
        for j in range(4):
            for i in range(4):
                place_y = (row_y - jnp.where(moved == 0, RING[j], RING[i])) & 3
                place_z = (row_z - jnp.where(moved == 0, RING[i], RING[j])) & 3
                owner = (place_y * 4 + place_z) * 2 + moved
                rows = pl.ds(pl.multiple_of(owner * 8, 8), 8)
                piece = pieces[4 * side + j]
                for s in range(LOC_C):
                    start = i * PIECE + s * 8
                    zero_ref[s, rows, :] = piece[start : start + 8, :]
                    start = start + STRIP
                    one_ref[s, rows, :] = piece[start : start + 8, :]

    wait(*range(9, 16))
    for side in range(2):
        moved = core if side == 0 else 1 - core
        for chip in range(N_CHIP):
            rows = pl.ds(pl.multiple_of((chip * 2 + moved) * 8, 8), 8)
            for head in range(3):
                for half in range(2):
                    start = (head * 2 + half) * 8
                    lanes = slice(half * 128, half * 128 + 128)
                    heads_ref[head, rows, lanes] = leads[side][chip, start : start + 8, :]
    inverse_one, inverse_zero = split(inverse_ref[1]), split(inverse_ref[0])
    cross_factor = heads_ref[1]
    mixer = split(dot3(dot_split(inverse_one, split(cross_factor)), inverse_ref[0]))

    def product(s, carry):
        hidden = jnp.logical_and(s == 0, is_zero | is_one)
        both = split(jnp.where(hidden, 0.0, matrix_ref[s]))
        panel_one = split(jnp.where(jnp.logical_and(is_one, s == 0), 0.0, one_ref[s]))
        panel_zero = split(zero_ref[s])
        product = dot_split(both, beside(panel_one, panel_zero))
        image_ref[0] += product[:, :BLK]
        image_ref[1] += product[:, BLK:]
        scaled = dot_split(panel_one, beside(inverse_one, mixer))
        scaled_zero = dot_split(panel_zero, inverse_zero) - scaled[:, BLK:]
        for place, panel in enumerate((scaled[:, :BLK], scaled_zero)):
            lanes = slice(place * BLK, place * BLK + BLK)
            high_ref[s, :, lanes], low_ref[s, :, lanes] = split(panel)
        return carry

    wait(0)
    image_ref[...] = jnp.zeros_like(image_ref)
    lax.fori_loop(0, LOC_C, product, 0)
    flush(1, 2)
    first = matrix_ref[0]
    image_one, image_zero = image_ref[0], image_ref[1]
    rest_one = jnp.where(is_one, first, 0.0) - image_one
    rest_zero = jnp.where(is_zero, first, 0.0) - image_zero
    scaled_one = dot_split(split(rest_one), inverse_one)
    rest_ref[0] = scaled_one
    rest_ref[1] = dot_split(split(rest_zero - dot3(scaled_one, cross_factor)), inverse_zero)
    flush(0)

    for d in range(4):
        kind = (col_place - d) & 3
        for s in range(LOC_C):
            rows = pl.ds(pl.multiple_of((4 * s + kind) * 8, 8), 8)
            for panel in range(2):
                tile = panels[d][panel, s * 8 : s * 8 + 8, :]
                if s == 0:
                    tile = jnp.where(kind < 2, 0.0, tile)
                left_ref[panel, rows, :] = tile
    row = lax.broadcasted_iota(jnp.int32, (BLK, BLK), 0)
    column = lax.broadcasted_iota(jnp.int32, (BLK, BLK), 1)

    def lower(value):
        return jnp.where(row >= column, value, 0.0)

    def phi(value):
        return jnp.where(row > column, value, jnp.where(row == column, 0.5 * value, 0.0))

    def spread(square, part):
        square_ref[...] = square
        square_ref[mine, :] += part
        return square_ref[...]

    def corner(square, factor, inverse):
        inner = phi(dot3t(factor, lower(square)))
        whole = dot3(dot3t(inverse, inner), inverse)
        return whole + whole.T

    def put(place, value):
        for half in range(2):
            tile = value[:, half * 128 : half * 128 + 128].reshape(N_CHIP, 2, RSUB, 128)
            rows = slice((place * 2 + half) * 8, (place * 2 + half) * 8 + 8)
            keep_ref[:, rows, :] = jnp.where(core == 0, tile[:, 0], tile[:, 1])
            give_ref[:, rows, :] = jnp.where(core == 0, tile[:, 1], tile[:, 0])

    left_one = split(left_ref[1].T)
    left_zero = split(left_ref[0].T)
    parts_one = split(image_one)
    parts_zero = split(image_zero)
    parts_rest = split(rest_one)
    inverse_one, inverse_zero = inverse_ref[1], inverse_ref[0]
    sum_one = dot_split(left_one, parts_rest) - dot_split(left_one, parts_one).T
    corner_one = corner(
        spread(-dot3(sum_one, inverse_one), jnp.where(is_one, first[8:16], 0.0)),
        heads_ref[0],
        inverse_one,
    )
    put(2, corner_one)
    sum_cross = dot_split(left_zero, parts_rest).T - dot_split(left_one, parts_zero)
    mixed = spread(dot3t(inverse_one, sum_cross), image_zero[8:16])
    cross = spread(
        -(mixed + dot3(corner_one, cross_factor)), jnp.where(is_zero, first[8:16], 0.0)
    )
    cross = dot3(cross, inverse_zero)
    put(0, cross)
    put(3, cross.T)
    sum_zero = dot_split(left_zero, split(rest_zero)) - dot_split(left_zero, parts_zero).T
    sum_zero = dot3(sum_zero - dot3t(mixed, cross_factor), inverse_zero)
    corner_zero = corner(
        spread(-(sum_zero + dot3t(cross_factor, cross)), jnp.where(is_zero, first[0:8], 0.0)),
        heads_ref[2],
        inverse_zero,
    )
    put(1, corner_zero)
    flush(3, 4)


def image_body(
    place_ref, staged, wait, made, flush, arrived_ref, both_ref, strips_ref, in_sem
):
    source_ref, rest_ref, high_ref, low_ref = staged
    chunk_refs = made
    col_place = place_ref[4]
    arriving = [
        pltpu.make_async_copy(source_ref.at[:, col], arrived_ref.at[col], in_sem.at[col])
        for col in range(N_COL)
    ]
    for copy in arriving:
        copy.start()
    wait(None)
    for col in range(N_COL):
        arriving[col].wait()

        def turn(low, carry):
            for half in range(2):
                tiles = mirror_tiles(arrived_ref.at[col], low, half)
                for (high, group), tile in tiles.items():
                    inner = 4 * high + low
                    if group == 0 and col < 2:
                        tile = jnp.zeros_like(tile)
                    if high == 0:
                        tile = jnp.where(jnp.logical_and(col_place == 0, low == 0), 0.0, tile)
                    rows = slice((4 * group + col) * 8, (4 * group + col) * 8 + 8)
                    both_ref[inner, rows, half * 128 : half * 128 + 128] = tile
            return carry

        lax.fori_loop(0, 4, turn, 0, unroll=2)
    wait(1, 2, 3)
    for part in range(2):
        blocks = range(part * 4, part * 4 + 4)
        pairs = [split(both_ref[s]) for s in blocks]
        left = [pair[0] for pair in pairs] * 2 + [pair[1] for pair in pairs]
        right = [high_ref[s] for s in blocks] + [low_ref[s] for s in blocks]
        right += [high_ref[s] for s in blocks]
        product = jnp.dot(
            jnp.concatenate(left, axis=1),
            jnp.concatenate(right, axis=0),
            preferred_element_type=F32,
        )
        for panel in range(2):
            lanes = slice(panel * BLK, panel * BLK + BLK)
            base = rest_ref[panel] if part == 0 else strips_ref[:, lanes]
            strips_ref[:, lanes] = base - product[:, lanes]
    for d in range(4):
        kind = (col_place + d) & 3
        for s in range(LOC_C):
            tile = strips_ref[pl.ds(pl.multiple_of((4 * s + kind) * 8, 8), 8), :]
            if s == 0:
                tile = jnp.where(kind < 2, 0.0, tile)
            chunk_refs[d][s * 8 : s * 8 + 8, :] = tile
        flush(d)


def total_body(place_ref, staged, wait, made, flush):
    wait(0)
    made[0][...] = jnp.sum(staged[0][...], axis=0)
    flush(0)


def strip_body(place_ref, staged, wait, made, flush):
    across_ref, *out_refs = made
    totals_ref = staged[4]
    col_place = place_ref[4]
    wait(*range(4))
    strip = (staged[0][...] + staged[1][...]) + (staged[2][...] + staged[3][...])
    for half in range(2):
        tiles = [
            strip[s * 8 : s * 8 + 8, k * BLK + half * 128 : k * BLK + half * 128 + 128]
            for s in range(LOC_C)
            for k in range(2)
        ]
        for sub, tile in enumerate(swap_groups(tiles)):
            across_ref[half * 16 + sub] = tile
    flush(0)
    wait(4)
    for d in range(4):
        target = (col_place + d) & 3
        out_refs[d][:STRIP] = jnp.where(target == 0, strip[:, BLK:], strip[:, :BLK])
        for mat in range(2):
            for half in range(2):
                start = mat * 16 + half * 8
                tile = jnp.where(
                    target == 0, totals_ref[start : start + 8], totals_ref[start + 32 : start + 40]
                )
                rows = slice(STRIP + mat * 8, STRIP + mat * 8 + 8)
                out_refs[d][rows, half * 128 : half * 128 + 128] = tile
        flush(1 + d)


def finish_body(
    place_ref, staged, wait, made, flush, top_ref, edge_ref, head_ref, edge_sem, out_sem
):
    half_ref, lines_ref, first_ref, across_ref = staged[:4]
    strips = staged[4:8]
    (out_ref,) = made
    edge = half_ref.at[:, pl.ds(0, 8), :]
    reading = pltpu.make_async_copy(edge, edge_ref, edge_sem)
    reading.start()
    col_place = place_ref[4]
    is_zero = col_place == 0
    is_one = col_place == 1
    owner = col_place < 2
    wait(1, 3)
    for half in range(2):
        turned = across_ref[half * 16 : half * 16 + 16].reshape(128, 128).T
        for s in range(LOC_C):
            for k in range(2):
                top_ref[k, s, half] = turned[(s * 2 + k) * 8 : (s * 2 + k) * 8 + 8]
    for s in range(1, LOC_C):
        for half in range(2):
            for block in range(2):
                rows = pl.ds(block * 128 + s * 2 + half, 8, stride=16)
                new = lines_ref[rows, :] + top_ref[1 - block, s, half]
                head_ref[block * 8 : block * 8 + 8, s * 2 + half, :] = 0.5 * new
    reading.wait()
    wait(2, 4, 5, 6, 7)
    for half in range(2):
        lanes = slice(half * 128, half * 128 + 128)
        part_a, part_b = [
            (strips[0][rows, lanes] + strips[1][rows, lanes])
            + (strips[2][rows, lanes] + strips[3][rows, lanes])
            for rows in (slice(STRIP, STRIP + 8), slice(STRIP + 8, STRIP + 16))
        ]
        own = lines_ref[pl.ds(half, 8, stride=16), :]
        head_ref[0:8, half, :] = 0.5 * jnp.where(
            is_zero, part_b, own + jnp.where(is_one, part_b, top_ref[1, 0, half])
        )
        own = lines_ref[pl.ds(128 + half, 8, stride=16), :]
        head_ref[8:16, half, :] = jnp.where(
            is_zero,
            edge_ref[8:16, half, :] + 0.5 * (part_a - own),
            0.5 * jnp.where(is_one, part_a, own + top_ref[0, 0, half]),
        )
        for d in range(4):
            kind = (col_place - d) & 3
            for s in range(LOC_C):
                rows = pl.ds(pl.multiple_of((4 * s + kind) * 8, 8), 8)
                change = 0.5 * (strips[d][s * 8 : s * 8 + 8, lanes] - first_ref[rows, lanes])
                edge_ref[rows, half, :] += jnp.where(owner, change, 0.0)
    writing = [
        pltpu.make_async_copy(head_ref, out_ref.at[pl.ds(0, 16)], out_sem.at[0]),
        pltpu.make_async_copy(
            edge_ref.at[pl.ds(16, ROWS - 16)],
            out_ref.at[pl.ds(16, ROWS - 16), pl.ds(0, 8), :],
            out_sem.at[1],
        ),
    ]
    for copy in writing:
        copy.start()
    for copy in writing:
        copy.wait()


def ring(first, d):
    pairs = []
    for i in range(N_ROW):
        y, z, core = i >> 3, (i >> 1) & 3, i & 1
        if (core == 0) == first:
            z = (z + d) & 3
        else:
            y = (y + d) & 3
        pairs.append((i, (y * 4 + z) * 2 + core))
    return pairs


def around(piece, first):
    return [piece] + [lax.ppermute(piece, "row", ring(first, d)) for d in RING[1:]]


def to_owners(pieces):
    moved = [
        lax.ppermute(pieces[d], "col", [((t - d) % 4, t) for t in range(2)]) for d in range(1, 4)
    ]
    return [pieces[0]] + moved


def on_device(adjoint, lower_panels, diag_inverse):
    row_place = lax.axis_index("row")
    col_place = lax.axis_index("col")
    place = jnp.stack(
        [row_place, row_place >> 3, (row_place >> 1) & 3, row_place & 1, col_place]
    ).astype(jnp.int32)
    lines = adjoint.reshape(LINES, 128)
    panels = lower_panels.reshape(2, STRIP, BLK)
    by_rows = [panels] + [
        lax.ppermute(panels, "col", [(i, (i + d) % 4) for i in range(4)]) for d in range(1, 4)
    ]
    lead = jnp.stack([piece[:, :RSUB] for piece in by_rows])
    lead_one = lax.dynamic_index_in_dim(lead, (col_place - 1) & 3, 0, False)
    lead_zero = lax.dynamic_index_in_dim(lead, col_place, 0, False)
    lead = jnp.stack([lead_one[1], lead_one[0], lead_zero[0]]).reshape(3, RSUB, 2, 128)
    lead = lead.transpose(0, 2, 1, 3).reshape(1, 6 * RSUB, 128)
    across_core = [(i, i ^ 1) for i in range(N_ROW)]
    same_core = [[2 * chip + core for chip in range(N_CHIP)] for core in range(2)]

    def exchange(value):
        return lax.all_to_all(
            value, "row", split_axis=0, concat_axis=0, tiled=True, axis_index_groups=same_core
        )

    ring_one = jnp.concatenate(around(panels.reshape(PIECE, BLK), True), axis=0)
    plane = around(ring_one, False)
    leads = exchange(jnp.broadcast_to(lead, (N_CHIP, 6 * RSUB, 128)))
    later, ring_one = lax.optimization_barrier((place, ring_one))
    high_shape = shape(2, LINES // 2, 128)
    part_shape = shape(4, LINES // 4, 128)
    wide = shape(LOC_C, ROWS, BLK)
    outgoing, matrix = call(
        pack_body,
        [part_shape, wide],
        [high_shape],
        scratch=[
            pltpu.VMEM(high_shape.shape, F32),
            pltpu.VMEM((2, LOC_C, BLK, 128), F32),
            pltpu.VMEM(part_shape.shape, F32),
            pltpu.SemaphoreType.DMA((2,)),
            pltpu.SemaphoreType.DMA((4,)),
        ],
        raw_in=(0,),
        raw_out=(0,),
        size=2**24,
    )(later, lines.reshape(high_shape.shape))
    outgoing, *plane = lax.optimization_barrier((outgoing, *plane))
    arrived = lax.all_to_all(
        outgoing.reshape(N_ROW * N_COL, 32, 128), ("row", "col"), split_axis=0, concat_axis=0, tiled=True
    )
    plane = plane + [lax.ppermute(part, "row", across_core) for part in plane]
    leads = [leads, lax.ppermute(leads, "row", across_core)]

    direct_ins = [matrix, *plane, diag_inverse, *by_rows, *leads]
    split_shape = shape(LOC_C, BLK, 2 * BLK, dtype=BF16)
    square_shape = pltpu.VMEM((BLK, BLK), F32)
    pair_shape = pltpu.VMEM((2, BLK, BLK), F32)
    wide_shape = pltpu.VMEM((LOC_C, BLK, BLK), F32)
    rest, high, low, corners, given = call(
        direct_body,
        [
            shape(2, BLK, BLK), split_shape, split_shape,
            shape(N_CHIP, 64, 128), shape(N_CHIP, 64, 128),
        ],
        direct_ins,
        scratch=[wide_shape, wide_shape, pair_shape, pair_shape, square_shape, pltpu.VMEM((3, BLK, BLK), F32)],
        flops=2**33,
        size=2**24,
    )(place, *direct_ins)
    corners = exchange(corners + lax.ppermute(given, "row", across_core))
    arrived = arrived.reshape(N_ROW, N_COL, 32, 128)
    image_ins = [arrived, rest, high, low]
    chunks = call(
        image_body,
        [shape(STRIP, 2 * BLK)] * 4,
        image_ins,
        scratch=[
            pltpu.VMEM((N_COL, N_ROW, 32, 128), F32),
            wide_shape,
            pltpu.VMEM((ROWS, 2 * BLK), F32),
            pltpu.SemaphoreType.DMA((N_COL,)),
        ],
        raw_in=(0,),
        eager=False,
        flops=2**32,
        size=2**24,
    )(place, *image_ins)
    strips = [chunks[0]] + [
        lax.ppermute(chunks[d], "col", [(i, (i + d) % 4) for i in range(4)]) for d in range(1, 4)
    ]
    corners, first, *chunks = lax.optimization_barrier((corners, matrix[0], *chunks))
    totals = call(total_body, [shape(64, 128)], [corners], near=(0,), size=2**19)(place, corners)
    strip_ins = [*strips, *totals]
    across, *panels = call(
        strip_body,
        [shape(N_ROW, RSUB, 128)] + [shape(STRIP + 2 * RSUB, BLK)] * 4,
        strip_ins,
        near=(1, 2, 3),
        size=2**21,
    )(place, *strip_ins)
    arrived, across = lax.optimization_barrier((arrived, across))
    across = lax.all_to_all(across, "row", split_axis=0, concat_axis=0, tiled=True)
    panels = to_owners(panels)
    half = half_sum(lines, arrived).reshape(ROWS, 16, 128)
    finish_ins = [half, lines, first, across, *panels]
    (result,) = call(
        finish_body,
        [shape(ROWS, 16, 128)],
        finish_ins,
        scratch=[
            pltpu.VMEM((2, LOC_C, 2, RSUB, 128), F32),
            pltpu.VMEM((ROWS, 8, 128), F32),
            pltpu.VMEM((16, 16, 128), F32),
            pltpu.SemaphoreType.DMA,
            pltpu.SemaphoreType.DMA((2,)),
        ],
        heads={1: 2 * 128},
        near=(3, 5, 6, 7),
        raw_in=(0,),
        raw_out=(0,),
        aliases={1: 0},
        size=2**23,
    )(place, *finish_ins)
    return result.reshape(NBLK, 1, RSUB, LOC_C, 1, BLK)


def solution(mesh):
    return jax.shard_map(
        on_device,
        mesh=mesh,
        in_specs=(
            P(None, "row", None, None, "col", None),
            P(None, None, "col", "row", None, None),
            P(),
        ),
        out_specs=P(None, "row", None, None, "col", None),
        check_vma=False,
    )
```

profile of v0, /device:TPU:1, one launch (start us, length us, event | category | flops | bytes accessed | tf_op | source)
XLA Modules:
  0.0 118.6 jit_solution(10954347583583838420)
XLA Ops:
  0.0 3.7 %collective-permute-start.2 = (f32[128,256]{1,0:T(8,128)}, f32[128,256]{1,0:T(8,128)S(1)}, u32[]{:S(2)}, u32[]{:S(2)}) collective-permute-start(f32[128,256]{1,0:T(8,128)} %bitcast.40), channel_id=1, source_target_pairs={{0,16},{4,68},{8,24},{12,76},{16,0},{20,84},{24,8},{28,92},{32,48}... | collective-permute-start | bytes 393224 | tf_op jit(solution)/shard_map/ppermute | solution.py:536
  5.2 1.2 %collective-permute-start.10 = (f32[2,64,256]{2,1,0:T(8,128)}, f32[2,64,256]{2,1,0:T(8,128)S(1)}, u32[]{:S(2)}, u32[]{:S(2)}) collective-permute-start(f32[2,64,256]{2,1,0:T(8,128)} %bitcast.43), channel_id=1, source_target_pairs={{0,1},{1,2},{2,3},{3,0},{4,5},{5,6},{6,7},{7,4},{8,9},{9,10},{10,1... | collective-permute-start | bytes 393224 | tf_op jit(solution)/shard_map/ppermute | solution.py:555
  6.4 1.5 %collective-permute-start.12 = (f32[2,64,256]{2,1,0:T(8,128)}, f32[2,64,256]{2,1,0:T(8,128)S(1)}, u32[]{:S(2)}, u32[]{:S(2)}) collective-permute-start(f32[2,64,256]{2,1,0:T(8,128)} %bitcast.44), channel_id=1, source_target_pairs={{0,3},{1,0},{2,1},{3,2},{4,7},{5,4},{6,5},{7,6},{8,11},{9,8},{10,9... | collective-permute-start | bytes 393224 | tf_op jit(solution)/shard_map/ppermute | solution.py:555
  8.6 1.5 %collective-permute-start.11 = (f32[2,64,256]{2,1,0:T(8,128)}, f32[2,64,256]{2,1,0:T(8,128)S(1)}, u32[]{:S(2)}, u32[]{:S(2)}) collective-permute-start(f32[2,64,256]{2,1,0:T(8,128)} %bitcast.46), channel_id=1, source_target_pairs={{0,2},{1,3},{2,0},{3,1},{4,6},{5,7},{6,4},{7,5},{8,10},{9,11},{10,... | collective-permute-start | bytes 393224 | tf_op jit(solution)/shard_map/ppermute | solution.py:555
  10.2 1.0 pad_maximum_fusion.refs_2_
  11.2 1.7 %collective-permute-start.3 = (f32[512,256]{1,0:T(8,128)S(1)}, f32[512,256]{1,0:T(8,128)S(1)}, u32[]{:S(2)}, u32[]{:S(2)}) collective-permute-start(f32[512,256]{1,0:T(8,128)S(1)} %pad_maximum_fusion.refs_2_), channel_id=1, source_target_pairs={{0,32},{4,12},{8,40},{12,20},{16,48},{20,28},{24,56},{28,4},{32,64... | collective-permute-start | bytes 1572872 | tf_op jit(solution)/shard_map/ppermute | solution.py:536
  12.9 2.2 %collective-permute-start.4 = (f32[512,256]{1,0:T(8,128)S(1)}, f32[512,256]{1,0:T(8,128)}, u32[]{:S(2)}, u32[]{:S(2)}) collective-permute-start(f32[512,256]{1,0:T(8,128)S(1)} %pad_maximum_fusion.refs_2_), channel_id=1, source_target_pairs={{0,96},{4,28},{8,104},{12,4},{16,112},{20,12},{24,120},{28,20},{32... | collective-permute-start | bytes 1572872 | tf_op jit(solution)/shard_map/ppermute | solution.py:536
  15.1 1.2 %collective-permute-start.5 = (f32[512,256]{1,0:T(8,128)S(1)}, f32[512,256]{1,0:T(8,128)}, u32[]{:S(2)}, u32[]{:S(2)}) collective-permute-start(f32[512,256]{1,0:T(8,128)S(1)} %pad_maximum_fusion.refs_2_), channel_id=1, source_target_pairs={{0,64},{4,20},{8,72},{12,28},{16,80},{20,4},{24,88},{28,12},{32,96... | collective-permute-start | bytes 1572872 | tf_op jit(solution)/shard_map/ppermute | solution.py:536
  17.2 5.2 %all-to-all-start.1 = ((f32[16,48,128]{2,1,0:T(8,128)}), f32[16,48,128]{2,1,0:T(8,128)S(1)}, u32[]{:S(2)}, u32[]{:S(2)}) async-start(f32[16,48,128]{2,1,0:T(8,128)} %broadcast_in_dim.8), calls=%async_computation.1 | async-start | bytes 786432 | tf_op jit(solution)/shard_map/all_to_all | solution.py:566
  23.1 5.1 %shard_map.37 = (f32[4,1024,128]{2,1,0:T(8,128)}, f32[8,256,256]{2,1,0:T(8,128)}) custom-call(s32[5]{0:T(128)} %stack.47.refs_0_, f32[2,2048,128]{2,1,0:T(8,128)} %bitcast.33), custom_call_target="tpu_custom_call" | custom-call | bytes 16777216 | tf_op jit(solution)/shard_map/pallas_call | solution.py:577
  28.8 5.9 %all-to-all-done.1.refs_15_ = f32[16,48,128]{2,1,0:T(8,128)S(1)} async-done(((f32[16,48,128]{2,1,0:T(8,128)}), f32[16,48,128]{2,1,0:T(8,128)S(1)}, u32[]{:S(2)}, u32[]{:S(2)}) %all-to-all-start.1) | async-done | bytes 393248 | tf_op jit(solution)/shard_map/all_to_all | solution.py:566
  34.8 7.7 %all-to-all-start = ((f32[128,32,128]{2,1,0:T(8,128)}), f32[128,32,128]{2,1,0:T(8,128)S(1)}, u32[]{:S(2)}, u32[]{:S(2)}) async-start(f32[128,32,128]{2,1,0:T(8,128)} %bitcast.39), calls=%async_computation | async-start | bytes 4194304 | tf_op jit(solution)/shard_map/all_to_all | solution.py:593
  42.5 1.1 collective-permute-start.6
  44.6 2.4 %collective-permute-done.13.refs_16_ = f32[16,48,128]{2,1,0:T(8,128)S(1)} collective-permute-done((f32[16,48,128]{2,1,0:T(8,128)S(1)}, f32[16,48,128]{2,1,0:T(8,128)S(1)}, u32[]{:S(2)}, u32[]{:S(2)}) %collective-permute-start.13) | collective-permute-done | bytes 393248 | tf_op jit(solution)/shard_map/ppermute | solution.py:597
  49.0 16.4 %shard_map.38 = (f32[2,256,256]{2,1,0:T(8,128)}, bf16[8,256,512]{2,1,0:T(8,128)(2,1)}, bf16[8,256,512]{2,1,0:T(8,128)(2,1)}, f32[16,64,128]{2,1,0:T(8,128)}, f32[16,64,128]{2,1,0:T(8,128)}) custom-call(s32[5]{0:T(128)} %stack.47.refs_0_, f32[8,256,256]{2,1,0:T(8,128)} %get-tuple-element.34.refs_1_, f32[512,256]{1,0:T(8,128)} %copy-done.4, ...), custom_call_target="tpu_custom_call" | custom-call | flops 8589934592 | bytes 16777216 | tf_op jit(solution)/shard_map/pallas_call | solution.py:604
  65.9 1.8 %collective-permute-done.17 = f32[16,64,128]{2,1,0:T(8,128)S(1)} collective-permute-done((f32[16,64,128]{2,1,0:T(8,128)}, f32[16,64,128]{2,1,0:T(8,128)S(1)}, u32[]{:S(2)}, u32[]{:S(2)}) %collective-permute-start.17) | collective-permute-done | bytes 524320 | tf_op jit(solution)/shard_map/ppermute | solution.py:615
  67.6 1.9 %add.13 = f32[16,64,128]{2,1,0:T(8,128)} add(f32[16,64,128]{2,1,0:T(8,128)} %get-tuple-element.46, f32[16,64,128]{2,1,0:T(8,128)S(1)} %collective-permute-done.17) | non-fusion elementwise | flops 131072 | bytes 1572864 | tf_op jit(solution)/shard_map/add | solution.py:615
  69.5 3.9 %all-to-all-done = f32[128,32,128]{2,1,0:T(8,128)S(1)} async-done(((f32[128,32,128]{2,1,0:T(8,128)}), f32[128,32,128]{2,1,0:T(8,128)S(1)}, u32[]{:S(2)}, u32[]{:S(2)}) %all-to-all-start) | async-done | bytes 2097184 | tf_op jit(solution)/shard_map/all_to_all | solution.py:593
  73.5 3.8 %all-to-all-start.2 = ((f32[16,64,128]{2,1,0:T(8,128)}), f32[16,64,128]{2,1,0:T(8,128)S(1)}, u32[]{:S(2)}, u32[]{:S(2)}) async-start(f32[16,64,128]{2,1,0:T(8,128)} %add.13), calls=%async_computation.2 | async-start | bytes 1048576 | tf_op jit(solution)/shard_map/all_to_all | solution.py:566
  77.2 6.5 %shard_map.39 = (f32[64,512]{1,0:T(8,128)}, f32[64,512]{1,0:T(8,128)}, f32[64,512]{1,0:T(8,128)}, f32[64,512]{1,0:T(8,128)}) custom-call(s32[5]{0:T(128)} %stack.47.refs_0_, f32[32,4,32,128]{3,2,1,0:T(8,128)} %bitcast.36, f32[2,256,256]{2,1,0:T(8,128)} %get-tuple-element.39.refs_2_, bf16[8,256,512]{2,1,0:T(8,128)(2,1)} %get-tuple-element.40.refs_3_, ...), custom_call_target="tpu_custom_call" | custom-call | flops 4294967296 | bytes 16777216 | tf_op jit(solution)/shard_map/pallas_call | solution.py:618
  84.1 2.2 %collective-permute-start.15 = (f32[64,512]{1,0:T(8,128)}, f32[64,512]{1,0:T(8,128)S(1)}, u32[]{:S(2)}, u32[]{:S(2)}) collective-permute-start(f32[64,512]{1,0:T(8,128)} %get-tuple-element.44), channel_id=1, source_target_pairs={{0,2},{1,3},{2,0},{3,1},{4,6},{5,7},{6,4},{7,5},{8,10},{9,11},{10,... | collective-permute-start | bytes 393224 | tf_op jit(solution)/shard_map/ppermute | solution.py:634
  86.3 1.2 collective-permute-start.16
  87.5 1.0 slice_bitcast_fusion.refs_3_
  89.1 1.6 %collective-permute-done.14.refs_2_ = f32[64,512]{1,0:T(8,128)S(1)} collective-permute-done((f32[64,512]{1,0:T(8,128)}, f32[64,512]{1,0:T(8,128)S(1)}, u32[]{:S(2)}, u32[]{:S(2)}) %collective-permute-start.14) | collective-permute-done | bytes 131104 | tf_op jit(solution)/shard_map/ppermute | solution.py:634
  90.7 1.5 %collective-permute-done.15.refs_3_ = f32[64,512]{1,0:T(8,128)S(1)} collective-permute-done((f32[64,512]{1,0:T(8,128)}, f32[64,512]{1,0:T(8,128)S(1)}, u32[]{:S(2)}, u32[]{:S(2)}) %collective-permute-start.15) | collective-permute-done | bytes 131104 | tf_op jit(solution)/shard_map/ppermute | solution.py:634
  94.1 1.8 %shard_map.41 = (f32[32,8,128]{2,1,0:T(8,128)}, f32[80,256]{1,0:T(8,128)S(1)}, f32[80,256]{1,0:T(8,128)S(1)}, f32[80,256]{1,0:T(8,128)S(1)}, f32[80,256]{1,0:T(8,128)S(1)}) custom-call(s32[5]{0:T(128)S(1)} %copy-done.2, f32[64,512]{1,0:T(8,128)S(1)} %copy-done.1, f32[64,512]{1,0:T(8,128)S(1)} %collective-permute-done.14.refs_2_, ...), custom_call_target="tpu_custom_call" | custom-call | bytes 2097152 | tf_op jit(solution)/shard_map/pallas_call | solution.py:639
  95.9 8.3 %all-to-all-start.3 = ((f32[32,8,128]{2,1,0:T(8,128)}), f32[32,8,128]{2,1,0:T(8,128)S(1)}, u32[]{:S(2)}, u32[]{:S(2)}) async-start(f32[32,8,128]{2,1,0:T(8,128)} %get-tuple-element.52), calls=%async_computation.3 | async-start | bytes 262144 | tf_op jit(solution)/shard_map/all_to_all | solution.py:647
  104.2 3.0 %collective-permute-start.18 = (f32[80,256]{1,0:T(8,128)S(1)}, f32[80,256]{1,0:T(8,128)S(1)}, u32[]{:S(2)}, u32[]{:S(2)}) collective-permute-start(f32[80,256]{1,0:T(8,128)S(1)} %get-tuple-element.54), channel_id=1, source_target_pairs={{3,0},{0,1},{7,4},{4,5},{11,8},{8,9},{15,12},{12,13},{19,16},{16,1... | collective-permute-start | bytes 245768 | tf_op jit(solution)/shard_map/ppermute | solution.py:541
  107.2 1.3 %collective-permute-start.19 = (f32[80,256]{1,0:T(8,128)S(1)}, f32[80,256]{1,0:T(8,128)S(1)}, u32[]{:S(2)}, u32[]{:S(2)}) collective-permute-start(f32[80,256]{1,0:T(8,128)S(1)} %get-tuple-element.55), channel_id=1, source_target_pairs={{2,0},{3,1},{6,4},{7,5},{10,8},{11,9},{14,12},{15,13},{18,16},{19,... | collective-permute-start | bytes 245768 | tf_op jit(solution)/shard_map/ppermute | solution.py:541
  108.5 1.3 %collective-permute-start.20 = (f32[80,256]{1,0:T(8,128)S(1)}, f32[80,256]{1,0:T(8,128)S(1)}, u32[]{:S(2)}, u32[]{:S(2)}) collective-permute-start(f32[80,256]{1,0:T(8,128)S(1)} %get-tuple-element.56), channel_id=1, source_target_pairs={{1,0},{2,1},{5,4},{6,5},{9,8},{10,9},{13,12},{14,13},{17,16},{18,1... | collective-permute-start | bytes 245768 | tf_op jit(solution)/shard_map/ppermute | solution.py:541
  109.8 5.0 %shard_map.42 = f32[8,4,128,128]{3,2,1,0:T(8,128)} custom-call(f32[8,4,128,128]{3,2,1,0:T(8,128)} %bitcast.34, f32[32,4,32,128]{3,2,1,0:T(8,128)} %bitcast.37), custom_call_target="tpu_custom_call" | custom-call | bytes 16777216 | tf_op jit(solution)/shard_map/pallas_call | solution.py:219
  114.9 3.6 %shard_map.43 = f32[256,16,128]{2,1,0:T(8,128)} custom-call(s32[5]{0:T(128)S(1)} %copy-done.2, f32[256,16,128]{2,1,0:T(8,128)} %bitcast.38, f32[4096,128]{1,0:T(8,128)S(1)} %bitcast.35, f32[256,256]{1,0:T(8,128)S(1)} %slice_bitcast_fusion.refs_3_, f32[32,8,128]{2,1,0:T(8,128)S(1)} %all-to-all-done.3.refs_4_, ...), custom_call_target="tpu_custom_call", output_to_operand_aliasing={{}: (1, {})} | custom-call | bytes 8388608 | tf_op jit(solution)/shard_map/pallas_call | solution.py:651
  (67 shorter events, 10.6 us)
Async XLA Ops:
  0.0 8.6 %collective-permute-start.2 = (f32[128,256]{1,0:T(8,128)}, f32[128,256]{1,0:T(8,128)S(1)}, u32[]{:S(2)}, u32[]{:S(2)}) collective-permute-start(f32[128,256]{1,0:T(8,128)} %bitcast.40), channel_id=1, source_target_pairs={{0,16},{4,68},{8,24},{12,76},{16,0},{20,84},{24,8},{28,92},{32,48}... | collective-permute-start | bytes 393224 | tf_op jit(solution)/shard_map/ppermute | solution.py:536
  3.7 6.4 %collective-permute-start.1 = (f32[128,256]{1,0:T(8,128)}, f32[128,256]{1,0:T(8,128)S(1)}, u32[]{:S(2)}, u32[]{:S(2)}) collective-permute-start(f32[128,256]{1,0:T(8,128)} %bitcast.41), channel_id=1, source_target_pairs={{0,24},{4,100},{8,0},{12,108},{16,8},{20,116},{24,16},{28,124},{32... | collective-permute-start | bytes 393224 | tf_op jit(solution)/shard_map/ppermute | solution.py:536
  4.5 5.7 %collective-permute-start = (f32[128,256]{1,0:T(8,128)}, f32[128,256]{1,0:T(8,128)S(1)}, u32[]{:S(2)}, u32[]{:S(2)}) collective-permute-start(f32[128,256]{1,0:T(8,128)} %bitcast.42), channel_id=1, source_target_pairs={{0,8},{4,36},{8,16},{12,44},{16,24},{20,52},{24,0},{28,60},{32,40}... | collective-permute-start | bytes 393224 | tf_op jit(solution)/shard_map/ppermute | solution.py:536
  5.2 11.1 %collective-permute-start.10 = (f32[2,64,256]{2,1,0:T(8,128)}, f32[2,64,256]{2,1,0:T(8,128)S(1)}, u32[]{:S(2)}, u32[]{:S(2)}) collective-permute-start(f32[2,64,256]{2,1,0:T(8,128)} %bitcast.43), channel_id=1, source_target_pairs={{0,1},{1,2},{2,3},{3,0},{4,5},{5,6},{6,7},{7,4},{8,9},{9,10},{10,1... | collective-permute-start | bytes 393224 | tf_op jit(solution)/shard_map/ppermute | solution.py:555
  6.4 8.7 %collective-permute-start.12 = (f32[2,64,256]{2,1,0:T(8,128)}, f32[2,64,256]{2,1,0:T(8,128)S(1)}, u32[]{:S(2)}, u32[]{:S(2)}) collective-permute-start(f32[2,64,256]{2,1,0:T(8,128)} %bitcast.44), channel_id=1, source_target_pairs={{0,3},{1,0},{2,1},{3,2},{4,7},{5,4},{6,5},{7,6},{8,11},{9,8},{10,9... | collective-permute-start | bytes 393224 | tf_op jit(solution)/shard_map/ppermute | solution.py:555
  8.6 7.7 %collective-permute-start.11 = (f32[2,64,256]{2,1,0:T(8,128)}, f32[2,64,256]{2,1,0:T(8,128)S(1)}, u32[]{:S(2)}, u32[]{:S(2)}) collective-permute-start(f32[2,64,256]{2,1,0:T(8,128)} %bitcast.46), channel_id=1, source_target_pairs={{0,2},{1,3},{2,0},{3,1},{4,6},{5,7},{6,4},{7,5},{8,10},{9,11},{10,... | collective-permute-start | bytes 393224 | tf_op jit(solution)/shard_map/ppermute | solution.py:555
  11.2 31.3 %copy-start.4 = (f32[512,256]{1,0:T(8,128)}, f32[512,256]{1,0:T(8,128)S(1)}, u32[]{:S(2)}) copy-start(f32[512,256]{1,0:T(8,128)S(1)} %pad_maximum_fusion.refs_2_) | copy-start | bytes 1572868
  11.2 17.0 %collective-permute-start.3 = (f32[512,256]{1,0:T(8,128)S(1)}, f32[512,256]{1,0:T(8,128)S(1)}, u32[]{:S(2)}, u32[]{:S(2)}) collective-permute-start(f32[512,256]{1,0:T(8,128)S(1)} %pad_maximum_fusion.refs_2_), channel_id=1, source_target_pairs={{0,32},{4,12},{8,40},{12,20},{16,48},{20,28},{24,56},{28,4},{32,64... | collective-permute-start | bytes 1572872 | tf_op jit(solution)/shard_map/ppermute | solution.py:536
  12.9 15.3 %collective-permute-start.4 = (f32[512,256]{1,0:T(8,128)S(1)}, f32[512,256]{1,0:T(8,128)}, u32[]{:S(2)}, u32[]{:S(2)}) collective-permute-start(f32[512,256]{1,0:T(8,128)S(1)} %pad_maximum_fusion.refs_2_), channel_id=1, source_target_pairs={{0,96},{4,28},{8,104},{12,4},{16,112},{20,12},{24,120},{28,20},{32... | collective-permute-start | bytes 1572872 | tf_op jit(solution)/shard_map/ppermute | solution.py:536
  15.1 19.7 %copy-start.7 = (f32[2,64,256]{2,1,0:T(8,128)}, f32[2,64,256]{2,1,0:T(8,128)S(1)}, u32[]{:S(2)}) copy-start(f32[2,64,256]{2,1,0:T(8,128)S(1)} %collective-permute-done.12.refs_14_) | copy-start | bytes 393220
  15.1 13.7 %collective-permute-start.5 = (f32[512,256]{1,0:T(8,128)S(1)}, f32[512,256]{1,0:T(8,128)}, u32[]{:S(2)}, u32[]{:S(2)}) collective-permute-start(f32[512,256]{1,0:T(8,128)S(1)} %pad_maximum_fusion.refs_2_), channel_id=1, source_target_pairs={{0,64},{4,20},{8,72},{12,28},{16,80},{20,4},{24,88},{28,12},{32,96... | collective-permute-start | bytes 1572872 | tf_op jit(solution)/shard_map/ppermute | solution.py:536
  16.3 18.4 %copy-start.8 = (f32[2,64,256]{2,1,0:T(8,128)}, f32[2,64,256]{2,1,0:T(8,128)S(1)}, u32[]{:S(2)}) copy-start(f32[2,64,256]{2,1,0:T(8,128)S(1)} %collective-permute-done.11.refs_13_) | copy-start | bytes 393220
  16.3 18.4 %copy-start.6 = (f32[2,64,256]{2,1,0:T(8,128)}, f32[2,64,256]{2,1,0:T(8,128)S(1)}, u32[]{:S(2)}) copy-start(f32[2,64,256]{2,1,0:T(8,128)S(1)} %collective-permute-done.10.refs_12_) | copy-start | bytes 393220
  17.2 17.6 %all-to-all-start.1 = ((f32[16,48,128]{2,1,0:T(8,128)}), f32[16,48,128]{2,1,0:T(8,128)S(1)}, u32[]{:S(2)}, u32[]{:S(2)}) async-start(f32[16,48,128]{2,1,0:T(8,128)} %broadcast_in_dim.8), calls=%async_computation.1 | async-start | bytes 786432 | tf_op jit(solution)/shard_map/all_to_all | solution.py:566
  28.2 6.5 %copy-start.9 = (f32[512,256]{1,0:T(8,128)}, f32[512,256]{1,0:T(8,128)S(1)}, u32[]{:S(2)}) copy-start(f32[512,256]{1,0:T(8,128)S(1)} %collective-permute-done.3.refs_3_) | copy-start | bytes 1572868
  34.7 9.5 %copy-start.5 = (f32[16,48,128]{2,1,0:T(8,128)}, f32[16,48,128]{2,1,0:T(8,128)S(1)}, u32[]{:S(2)}) copy-start(f32[16,48,128]{2,1,0:T(8,128)S(1)} %all-to-all-done.1.refs_15_) | copy-start | bytes 1179652
  34.8 38.7 %all-to-all-start = ((f32[128,32,128]{2,1,0:T(8,128)}), f32[128,32,128]{2,1,0:T(8,128)S(1)}, u32[]{:S(2)}, u32[]{:S(2)}) async-start(f32[128,32,128]{2,1,0:T(8,128)} %bitcast.39), calls=%async_computation | async-start | bytes 4194304 | tf_op jit(solution)/shard_map/all_to_all | solution.py:593
  42.5 4.6 %collective-permute-start.6 = (f32[512,256]{1,0:T(8,128)S(1)}, f32[512,256]{1,0:T(8,128)S(1)}, u32[]{:S(2)}, u32[]{:S(2)}) collective-permute-start(f32[512,256]{1,0:T(8,128)S(1)} %pad_maximum_fusion.refs_2_), channel_id=1, source_target_pairs={{0,4},{4,0},{8,12},{12,8},{16,20},{20,16},{24,28},{28,24},{32,36},... | collective-permute-start | bytes 1572872 | tf_op jit(solution)/shard_map/ppermute | solution.py:596
  43.6 3.4 %collective-permute-start.7 = (f32[512,256]{1,0:T(8,128)}, f32[512,256]{1,0:T(8,128)S(1)}, u32[]{:S(2)}, u32[]{:S(2)}) collective-permute-start(f32[512,256]{1,0:T(8,128)} %copy-done.9), channel_id=1, source_target_pairs={{0,4},{4,0},{8,12},{12,8},{16,20},{20,16},{24,28},{28,24},{32,36},... | collective-permute-start | bytes 1572872 | tf_op jit(solution)/shard_map/ppermute | solution.py:596
  43.7 3.7 %collective-permute-start.8 = (f32[512,256]{1,0:T(8,128)}, f32[512,256]{1,0:T(8,128)S(1)}, u32[]{:S(2)}, u32[]{:S(2)}) collective-permute-start(f32[512,256]{1,0:T(8,128)} %collective-permute-done.4.refs_4_), channel_id=1, source_target_pairs={{0,4},{4,0},{8,12},{12,8},{16,20},{20,16},{24,28},{28,24},{32,36},... | collective-permute-start | bytes 1572872 | tf_op jit(solution)/shard_map/ppermute | solution.py:596
  44.1 4.0 %collective-permute-start.9 = (f32[512,256]{1,0:T(8,128)}, f32[512,256]{1,0:T(8,128)S(1)}, u32[]{:S(2)}, u32[]{:S(2)}) collective-permute-start(f32[512,256]{1,0:T(8,128)} %collective-permute-done.5.refs_5_), channel_id=1, source_target_pairs={{0,4},{4,0},{8,12},{12,8},{16,20},{20,16},{24,28},{28,24},{32,36},... | collective-permute-start | bytes 1572872 | tf_op jit(solution)/shard_map/ppermute | solution.py:596
  44.2 2.8 %collective-permute-start.13 = (f32[16,48,128]{2,1,0:T(8,128)S(1)}, f32[16,48,128]{2,1,0:T(8,128)S(1)}, u32[]{:S(2)}, u32[]{:S(2)}) collective-permute-start(f32[16,48,128]{2,1,0:T(8,128)S(1)} %all-to-all-done.1.refs_15_), channel_id=1, source_target_pairs={{0,4},{4,0},{8,12},{12,8},{16,20},{20,16},{24,28},{28,24},{32,36},... | collective-permute-start | bytes 1179656 | tf_op jit(solution)/shard_map/ppermute | solution.py:597
  65.4 2.2 %collective-permute-start.17 = (f32[16,64,128]{2,1,0:T(8,128)}, f32[16,64,128]{2,1,0:T(8,128)S(1)}, u32[]{:S(2)}, u32[]{:S(2)}) collective-permute-start(f32[16,64,128]{2,1,0:T(8,128)} %get-tuple-element.47), channel_id=1, source_target_pairs={{0,4},{4,0},{8,12},{12,8},{16,20},{20,16},{24,28},{28,24},{32,36},... | collective-permute-start | bytes 1572872 | tf_op jit(solution)/shard_map/ppermute | solution.py:615
  73.5 15.0 %all-to-all-start.2 = ((f32[16,64,128]{2,1,0:T(8,128)}), f32[16,64,128]{2,1,0:T(8,128)S(1)}, u32[]{:S(2)}, u32[]{:S(2)}) async-start(f32[16,64,128]{2,1,0:T(8,128)} %add.13), calls=%async_computation.2 | async-start | bytes 1048576 | tf_op jit(solution)/shard_map/all_to_all | solution.py:566
  77.2 11.2 %copy-start.2 = (s32[5]{0:T(128)S(1)}, s32[5]{0:T(128)}, u32[]{:S(2)}) copy-start(s32[5]{0:T(128)} %stack.47.refs_0_) | copy-start | bytes 64
  83.7 7.0 %collective-permute-start.14 = (f32[64,512]{1,0:T(8,128)}, f32[64,512]{1,0:T(8,128)S(1)}, u32[]{:S(2)}, u32[]{:S(2)}) collective-permute-start(f32[64,512]{1,0:T(8,128)} %get-tuple-element.43), channel_id=1, source_target_pairs={{0,1},{1,2},{2,3},{3,0},{4,5},{5,6},{6,7},{7,4},{8,9},{9,10},{10,1... | collective-permute-start | bytes 393224 | tf_op jit(solution)/shard_map/ppermute | solution.py:634
  84.1 8.1 %collective-permute-start.15 = (f32[64,512]{1,0:T(8,128)}, f32[64,512]{1,0:T(8,128)S(1)}, u32[]{:S(2)}, u32[]{:S(2)}) collective-permute-start(f32[64,512]{1,0:T(8,128)} %get-tuple-element.44), channel_id=1, source_target_pairs={{0,2},{1,3},{2,0},{3,1},{4,6},{5,7},{6,4},{7,5},{8,10},{9,11},{10,... | collective-permute-start | bytes 393224 | tf_op jit(solution)/shard_map/ppermute | solution.py:634
  86.3 6.8 %collective-permute-start.16 = (f32[64,512]{1,0:T(8,128)}, f32[64,512]{1,0:T(8,128)S(1)}, u32[]{:S(2)}, u32[]{:S(2)}) collective-permute-start(f32[64,512]{1,0:T(8,128)} %get-tuple-element.45), channel_id=1, source_target_pairs={{0,3},{1,0},{2,1},{3,2},{4,7},{5,4},{6,5},{7,6},{8,11},{9,8},{10,9... | collective-permute-start | bytes 393224 | tf_op jit(solution)/shard_map/ppermute | solution.py:634
  95.9 18.9 %all-to-all-start.3 = ((f32[32,8,128]{2,1,0:T(8,128)}), f32[32,8,128]{2,1,0:T(8,128)S(1)}, u32[]{:S(2)}, u32[]{:S(2)}) async-start(f32[32,8,128]{2,1,0:T(8,128)} %get-tuple-element.52), calls=%async_computation.3 | async-start | bytes 262144 | tf_op jit(solution)/shard_map/all_to_all | solution.py:647
  104.2 10.6 %collective-permute-start.18 = (f32[80,256]{1,0:T(8,128)S(1)}, f32[80,256]{1,0:T(8,128)S(1)}, u32[]{:S(2)}, u32[]{:S(2)}) collective-permute-start(f32[80,256]{1,0:T(8,128)S(1)} %get-tuple-element.54), channel_id=1, source_target_pairs={{3,0},{0,1},{7,4},{4,5},{11,8},{8,9},{15,12},{12,13},{19,16},{16,1... | collective-permute-start | bytes 245768 | tf_op jit(solution)/shard_map/ppermute | solution.py:541
  107.2 7.6 %collective-permute-start.19 = (f32[80,256]{1,0:T(8,128)S(1)}, f32[80,256]{1,0:T(8,128)S(1)}, u32[]{:S(2)}, u32[]{:S(2)}) collective-permute-start(f32[80,256]{1,0:T(8,128)S(1)} %get-tuple-element.55), channel_id=1, source_target_pairs={{2,0},{3,1},{6,4},{7,5},{10,8},{11,9},{14,12},{15,13},{18,16},{19,... | collective-permute-start | bytes 245768 | tf_op jit(solution)/shard_map/ppermute | solution.py:541
  108.5 6.3 %collective-permute-start.20 = (f32[80,256]{1,0:T(8,128)S(1)}, f32[80,256]{1,0:T(8,128)S(1)}, u32[]{:S(2)}, u32[]{:S(2)}) collective-permute-start(f32[80,256]{1,0:T(8,128)S(1)} %get-tuple-element.56), channel_id=1, source_target_pairs={{1,0},{2,1},{5,4},{6,5},{9,8},{10,9},{13,12},{14,13},{17,16},{18,1... | collective-permute-start | bytes 245768 | tf_op jit(solution)/shard_map/ppermute | solution.py:541
  (8 other events, 14.9 us)
where the time goes:
time: 120 us; the launch traced here: 119 us
  starting transfers between devices  51.4 us (43%)
  Pallas kernels  39.1 us (33%)
  waiting for transfers between devices  19.8 us (16%)
  local copies, waits for them, and re-layouts  4.95 us (4%)
  other arithmetic  2.92 us (2%)
    pallas_call x1, Pallas kernels, on_device(): call(direct_body, [shape(2, BLK, BLK), split_shape, split_shape, shape(N_...  16.4 us
    ppermute x6, starting transfers between devices, around(): lax.ppermute(piece, 'row', ring(first, d))  10.3 us
    all_to_all x2, starting transfers between devices, exchange(): lax.all_to_all(value, 'row', split_axis=0, concat_axis=0, tiled=True, axi...  8.94 us
    all_to_all x1, starting transfers between devices, on_device(): lax.all_to_all(across, 'row', split_axis=0, concat_axis=0, tiled=True)  8.3 us
    all_to_all x1, starting transfers between devices, on_device(): lax.all_to_all(outgoing.reshape(N_ROW * N_COL, 32, 128), ('row', 'col'),...  7.69 us
    pallas_call x1, Pallas kernels, on_device(): call(image_body, [shape(STRIP, 2 * BLK)] * 4, image_ins, scratch=[pltpu.V...  6.5 us
    all_to_all x2, waiting for transfers between devices, exchange(): lax.all_to_all(value, 'row', split_axis=0, concat_axis=0, tiled=True, axi...  5.93 us
    ppermute x3, starting transfers between devices, to_owners(): lax.ppermute(pieces[d], 'col', [((t - d) % 4, t) for t in range(2)])  5.54 us
  transfers between devices with their start and end apart: 25, of which 10 were waited for; matrix products, arithmetic and copies ran while one was open for 5% of the time, Pallas kernels for 28%

commit v1 on v0

--- a/solution.py
+++ b/solution.py
@@ -30,7 +30,7 @@
 
 
 def call(
-    body, outs, ins, scratch=(), heads=None, raw_in=(), raw_out=(), near=(), aliases=None, eager=True,
+    body, outs, ins, scratch=(), heads=None, raw_in=(), raw_out=(), near=(), limit=0, aliases=None, eager=True,
     flops=0, size=0,
 ):
     count, results = len(ins), len(outs)
@@ -95,7 +95,7 @@
         + list(scratch)
         + [pltpu.SemaphoreType.DMA((count,)), pltpu.SemaphoreType.DMA((results,))],
         input_output_aliases=aliases or {},
-        compiler_params=pltpu.CompilerParams(vmem_limit_bytes=SMALL_LIMIT if near else VMEM_LIMIT),
+        compiler_params=pltpu.CompilerParams(vmem_limit_bytes=limit or (SMALL_LIMIT if near else VMEM_LIMIT)),
         cost_estimate=pl.CostEstimate(flops=flops, bytes_accessed=size, transcendentals=0),
     )
 
@@ -608,6 +608,8 @@
             shape(N_CHIP, 64, 128), shape(N_CHIP, 64, 128),
         ],
         direct_ins,
+        near=(*range(1, 9), 11, 12, 13, 14, 15),
+        limit=50 * 2**20,
         scratch=[wide_shape, wide_shape, pair_shape, pair_shape, square_shape, pltpu.VMEM((3, BLK, BLK), F32)],
         flops=2**33,
         size=2**24,
@@ -640,7 +642,7 @@
         strip_body,
         [shape(N_ROW, RSUB, 128)] + [shape(STRIP + 2 * RSUB, BLK)] * 4,
         strip_ins,
-        near=(1, 2, 3),
+        near=(0, 1, 2, 3, 4),
         size=2**21,
     )(place, *strip_ins)
     arrived, across = lax.optimization_barrier((arrived, across))

time: 120 us -> 119 us (level)
  waiting for transfers between devices: 19.8 us -> 21.2 us
  Pallas kernels: 39.1 us -> 37.8 us
    unnamed x30 -> x24, local copies, waits for them, and re-layouts: 1.75 us -> 2.99 us
  transfers between devices with their start and end apart: 25 -> 25, of which waited for: 10 -> 7; matrix products, arithmetic and copies ran while one was open for 5% -> 4% of each run, Pallas kernels for 28% -> 28%
where the time goes in v1:
time: 119 us; the launch traced here: 118 us
  starting transfers between devices  50.3 us (42%)
  Pallas kernels  37.8 us (32%)
  waiting for transfers between devices  21.2 us (18%)
  local copies, waits for them, and re-layouts  6.1 us (5%)
  other arithmetic  1.88 us (2%)
    pallas_call x1, Pallas kernels, on_device(): call(direct_body, [shape(2, BLK, BLK), split_shape, split_shape, shape(N_...  15.4 us
    ppermute x6, starting transfers between devices, around(): lax.ppermute(piece, 'row', ring(first, d))  10.3 us
    all_to_all x2, starting transfers between devices, exchange(): lax.all_to_all(value, 'row', split_axis=0, concat_axis=0, tiled=True, axi...  8.94 us
    all_to_all x1, starting transfers between devices, on_device(): lax.all_to_all(across, 'row', split_axis=0, concat_axis=0, tiled=True)  8.29 us
    all_to_all x1, starting transfers between devices, on_device(): lax.all_to_all(outgoing.reshape(N_ROW * N_COL, 32, 128), ('row', 'col'),...  8.15 us
    pallas_call x1, Pallas kernels, on_device(): call(image_body, [shape(STRIP, 2 * BLK)] * 4, image_ins, scratch=[pltpu.V...  6.49 us
    all_to_all x2, waiting for transfers between devices, exchange(): lax.all_to_all(value, 'row', split_axis=0, concat_axis=0, tiled=True, axi...  6.01 us
    pallas_call x1, Pallas kernels, on_device(): call(pack_body, [part_shape, wide], [high_shape], scratch=[pltpu.VMEM(hig...  5.12 us
  transfers between devices with their start and end apart: 25, of which 7 were waited for; matrix products, arithmetic and copies ran while one was open for 4% of the time, Pallas kernels for 28%

profile of v1, /device:TPU:1, one launch (start us, length us, event | category | flops | bytes accessed | tf_op | source)
XLA Modules:
  0.0 117.7 jit_solution(2567555578798715714)
XLA Ops:
  0.0 3.7 %collective-permute-start.2 = (f32[128,256]{1,0:T(8,128)}, f32[128,256]{1,0:T(8,128)S(1)}, u32[]{:S(2)}, u32[]{:S(2)}) collective-permute-start(f32[128,256]{1,0:T(8,128)} %bitcast.36), channel_id=1, source_target_pairs={{0,16},{4,68},{8,24},{12,76},{16,0},{20,84},{24,8},{28,92},{32,48}... | collective-permute-start | bytes 393224 | tf_op jit(solution)/shard_map/ppermute | solution.py:536
  5.2 1.2 %collective-permute-start.10 = (f32[2,64,256]{2,1,0:T(8,128)}, f32[2,64,256]{2,1,0:T(8,128)S(1)}, u32[]{:S(2)}, u32[]{:S(2)}) collective-permute-start(f32[2,64,256]{2,1,0:T(8,128)} %bitcast.39), channel_id=1, source_target_pairs={{0,1},{1,2},{2,3},{3,0},{4,5},{5,6},{6,7},{7,4},{8,9},{9,10},{10,1... | collective-permute-start | bytes 393224 | tf_op jit(solution)/shard_map/ppermute | solution.py:555
  6.4 1.5 %collective-permute-start.12 = (f32[2,64,256]{2,1,0:T(8,128)}, f32[2,64,256]{2,1,0:T(8,128)S(1)}, u32[]{:S(2)}, u32[]{:S(2)}) collective-permute-start(f32[2,64,256]{2,1,0:T(8,128)} %bitcast.40), channel_id=1, source_target_pairs={{0,3},{1,0},{2,1},{3,2},{4,7},{5,4},{6,5},{7,6},{8,11},{9,8},{10,9... | collective-permute-start | bytes 393224 | tf_op jit(solution)/shard_map/ppermute | solution.py:555
  8.6 1.5 %collective-permute-start.11 = (f32[2,64,256]{2,1,0:T(8,128)}, f32[2,64,256]{2,1,0:T(8,128)S(1)}, u32[]{:S(2)}, u32[]{:S(2)}) collective-permute-start(f32[2,64,256]{2,1,0:T(8,128)} %bitcast.42), channel_id=1, source_target_pairs={{0,2},{1,3},{2,0},{3,1},{4,6},{5,7},{6,4},{7,5},{8,10},{9,11},{10,... | collective-permute-start | bytes 393224 | tf_op jit(solution)/shard_map/ppermute | solution.py:555
  10.2 1.0 pad_maximum_fusion.refs_2_
  11.2 1.7 %collective-permute-start.3 = (f32[512,256]{1,0:T(8,128)S(1)}, f32[512,256]{1,0:T(8,128)S(1)}, u32[]{:S(2)}, u32[]{:S(2)}) collective-permute-start(f32[512,256]{1,0:T(8,128)S(1)} %pad_maximum_fusion.refs_2_), channel_id=1, source_target_pairs={{0,32},{4,12},{8,40},{12,20},{16,48},{20,28},{24,56},{28,4},{32,64... | collective-permute-start | bytes 1572872 | tf_op jit(solution)/shard_map/ppermute | solution.py:536
  12.9 2.2 %collective-permute-start.4 = (f32[512,256]{1,0:T(8,128)S(1)}, f32[512,256]{1,0:T(8,128)S(1)}, u32[]{:S(2)}, u32[]{:S(2)}) collective-permute-start(f32[512,256]{1,0:T(8,128)S(1)} %pad_maximum_fusion.refs_2_), channel_id=1, source_target_pairs={{0,96},{4,28},{8,104},{12,4},{16,112},{20,12},{24,120},{28,20},{32... | collective-permute-start | bytes 1572872 | tf_op jit(solution)/shard_map/ppermute | solution.py:536
  15.1 1.2 %collective-permute-start.5 = (f32[512,256]{1,0:T(8,128)S(1)}, f32[512,256]{1,0:T(8,128)S(1)}, u32[]{:S(2)}, u32[]{:S(2)}) collective-permute-start(f32[512,256]{1,0:T(8,128)S(1)} %pad_maximum_fusion.refs_2_), channel_id=1, source_target_pairs={{0,64},{4,20},{8,72},{12,28},{16,80},{20,4},{24,88},{28,12},{32,96... | collective-permute-start | bytes 1572872 | tf_op jit(solution)/shard_map/ppermute | solution.py:536
  17.1 5.2 %all-to-all-start.1 = ((f32[16,48,128]{2,1,0:T(8,128)}), f32[16,48,128]{2,1,0:T(8,128)S(1)}, u32[]{:S(2)}, u32[]{:S(2)}) async-start(f32[16,48,128]{2,1,0:T(8,128)} %broadcast_in_dim.8), calls=%async_computation.1 | async-start | bytes 786432 | tf_op jit(solution)/shard_map/all_to_all | solution.py:566
  22.9 5.1 %shard_map.37 = (f32[4,1024,128]{2,1,0:T(8,128)}, f32[8,256,256]{2,1,0:T(8,128)}) custom-call(s32[5]{0:T(128)} %stack.47.refs_0_, f32[2,2048,128]{2,1,0:T(8,128)} %bitcast.33), custom_call_target="tpu_custom_call" | custom-call | bytes 16777216 | tf_op jit(solution)/shard_map/pallas_call | solution.py:577
  28.7 6.0 %all-to-all-done.1.refs_15_ = f32[16,48,128]{2,1,0:T(8,128)S(1)} async-done(((f32[16,48,128]{2,1,0:T(8,128)}), f32[16,48,128]{2,1,0:T(8,128)S(1)}, u32[]{:S(2)}, u32[]{:S(2)}) %all-to-all-start.1) | async-done | bytes 393248 | tf_op jit(solution)/shard_map/all_to_all | solution.py:566
  34.7 8.1 %all-to-all-start = ((f32[128,32,128]{2,1,0:T(8,128)}), f32[128,32,128]{2,1,0:T(8,128)}, u32[]{:S(2)}, u32[]{:S(2)}) async-start(f32[128,32,128]{2,1,0:T(8,128)} %bitcast.46), calls=%async_computation | async-start | bytes 4194304 | tf_op jit(solution)/shard_map/all_to_all | solution.py:593
  42.9 1.2 %collective-permute-start.6 = (f32[512,256]{1,0:T(8,128)S(1)}, f32[512,256]{1,0:T(8,128)S(1)}, u32[]{:S(2)}, u32[]{:S(2)}) collective-permute-start(f32[512,256]{1,0:T(8,128)S(1)} %pad_maximum_fusion.refs_2_), channel_id=1, source_target_pairs={{0,4},{4,0},{8,12},{12,8},{16,20},{20,16},{24,28},{28,24},{32,36},... | collective-permute-start | bytes 1572872 | tf_op jit(solution)/shard_map/ppermute | solution.py:596
  45.1 3.3 %collective-permute-done.13.refs_16_ = f32[16,48,128]{2,1,0:T(8,128)S(1)} collective-permute-done((f32[16,48,128]{2,1,0:T(8,128)S(1)}, f32[16,48,128]{2,1,0:T(8,128)S(1)}, u32[]{:S(2)}, u32[]{:S(2)}) %collective-permute-start.13) | collective-permute-done | bytes 393248 | tf_op jit(solution)/shard_map/ppermute | solution.py:597
  49.8 15.4 %shard_map.38 = (f32[2,256,256]{2,1,0:T(8,128)S(1)}, bf16[8,256,512]{2,1,0:T(8,128)(2,1)}, bf16[8,256,512]{2,1,0:T(8,128)(2,1)}, f32[16,64,128]{2,1,0:T(8,128)S(1)}, f32[16,64,128]{2,1,0:T(8,128)S(1)}) custom-call(s32[5]{0:T(128)S(1)} %copy-done.3, f32[8,256,256]{2,1,0:T(8,128)} %get-tuple-element.34.refs_1_, f32[512,256]{1,0:T(8,128)S(1)} %pad_maximum_fusion.refs_2_, ...), custom_call_target="tpu_custom_call" | custom-call | flops 8589934592 | bytes 16777216 | tf_op jit(solution)/shard_map/pallas_call | solution.py:604
  66.3 1.5 %collective-permute-done.17 = f32[16,64,128]{2,1,0:T(8,128)S(1)} collective-permute-done((f32[16,64,128]{2,1,0:T(8,128)S(1)}, f32[16,64,128]{2,1,0:T(8,128)S(1)}, u32[]{:S(2)}, u32[]{:S(2)}) %collective-permute-start.17) | collective-permute-done | bytes 524320 | tf_op jit(solution)/shard_map/ppermute | solution.py:617
  67.9 0.9 add.13
  68.8 4.8 %all-to-all-done = f32[128,32,128]{2,1,0:T(8,128)} async-done(((f32[128,32,128]{2,1,0:T(8,128)}), f32[128,32,128]{2,1,0:T(8,128)}, u32[]{:S(2)}, u32[]{:S(2)}) %all-to-all-start) | async-done | bytes 2097184 | tf_op jit(solution)/shard_map/all_to_all | solution.py:593
  73.5 3.8 %all-to-all-start.2 = ((f32[16,64,128]{2,1,0:T(8,128)}), f32[16,64,128]{2,1,0:T(8,128)S(1)}, u32[]{:S(2)}, u32[]{:S(2)}) async-start(f32[16,64,128]{2,1,0:T(8,128)} %add.13), calls=%async_computation.2 | async-start | bytes 1048576 | tf_op jit(solution)/shard_map/all_to_all | solution.py:566
  77.3 6.5 %shard_map.39 = (f32[64,512]{1,0:T(8,128)}, f32[64,512]{1,0:T(8,128)}, f32[64,512]{1,0:T(8,128)}, f32[64,512]{1,0:T(8,128)}) custom-call(s32[5]{0:T(128)} %stack.47.refs_0_, f32[32,4,32,128]{3,2,1,0:T(8,128)} %bitcast.9.refs_1_.arrived_ref, f32[2,256,256]{2,1,0:T(8,128)} %copy-done.5, bf16[8,256,512]{2,1,0:T(8,128)(2,1)} %get-tuple-element.40.refs_3_, ...), custom_call_target="tpu_custom_call" | custom-call | flops 4294967296 | bytes 16777216 | tf_op jit(solution)/shard_map/pallas_call | solution.py:620
  84.2 1.4 %collective-permute-start.15 = (f32[64,512]{1,0:T(8,128)}, f32[64,512]{1,0:T(8,128)S(1)}, u32[]{:S(2)}, u32[]{:S(2)}) collective-permute-start(f32[64,512]{1,0:T(8,128)} %get-tuple-element.44), channel_id=1, source_target_pairs={{0,2},{1,3},{2,0},{3,1},{4,6},{5,7},{6,4},{7,5},{8,10},{9,11},{10,... | collective-permute-start | bytes 393224 | tf_op jit(solution)/shard_map/ppermute | solution.py:636
  85.6 1.2 collective-permute-start.16
  86.8 1.0 slice_bitcast_fusion.refs_3_
  88.4 4.6 %collective-permute-done.14.refs_2_ = f32[64,512]{1,0:T(8,128)S(1)} collective-permute-done((f32[64,512]{1,0:T(8,128)}, f32[64,512]{1,0:T(8,128)S(1)}, u32[]{:S(2)}, u32[]{:S(2)}) %collective-permute-start.14) | collective-permute-done | bytes 131104 | tf_op jit(solution)/shard_map/ppermute | solution.py:636
  93.3 0.9 copy-done.2
  94.2 1.6 %shard_map.41 = (f32[32,8,128]{2,1,0:T(8,128)}, f32[80,256]{1,0:T(8,128)S(1)}, f32[80,256]{1,0:T(8,128)S(1)}, f32[80,256]{1,0:T(8,128)S(1)}, f32[80,256]{1,0:T(8,128)S(1)}) custom-call(s32[5]{0:T(128)S(1)} %copy-done.4, f32[64,512]{1,0:T(8,128)S(1)} %copy-done.2, f32[64,512]{1,0:T(8,128)S(1)} %collective-permute-done.14.refs_2_, ...), custom_call_target="tpu_custom_call" | custom-call | bytes 2097152 | tf_op jit(solution)/shard_map/pallas_call | solution.py:641
  95.8 8.3 %all-to-all-start.3 = ((f32[32,8,128]{2,1,0:T(8,128)}), f32[32,8,128]{2,1,0:T(8,128)S(1)}, u32[]{:S(2)}, u32[]{:S(2)}) async-start(f32[32,8,128]{2,1,0:T(8,128)} %get-tuple-element.52), calls=%async_computation.3 | async-start | bytes 262144 | tf_op jit(solution)/shard_map/all_to_all | solution.py:649
  104.1 2.2 %collective-permute-start.18 = (f32[80,256]{1,0:T(8,128)S(1)}, f32[80,256]{1,0:T(8,128)S(1)}, u32[]{:S(2)}, u32[]{:S(2)}) collective-permute-start(f32[80,256]{1,0:T(8,128)S(1)} %get-tuple-element.54), channel_id=1, source_target_pairs={{3,0},{0,1},{7,4},{4,5},{11,8},{8,9},{15,12},{12,13},{19,16},{16,1... | collective-permute-start | bytes 245768 | tf_op jit(solution)/shard_map/ppermute | solution.py:541
  106.2 1.3 %collective-permute-start.19 = (f32[80,256]{1,0:T(8,128)S(1)}, f32[80,256]{1,0:T(8,128)S(1)}, u32[]{:S(2)}, u32[]{:S(2)}) collective-permute-start(f32[80,256]{1,0:T(8,128)S(1)} %get-tuple-element.55), channel_id=1, source_target_pairs={{2,0},{3,1},{6,4},{7,5},{10,8},{11,9},{14,12},{15,13},{18,16},{19,... | collective-permute-start | bytes 245768 | tf_op jit(solution)/shard_map/ppermute | solution.py:541
  107.5 1.3 %collective-permute-start.20 = (f32[80,256]{1,0:T(8,128)S(1)}, f32[80,256]{1,0:T(8,128)S(1)}, u32[]{:S(2)}, u32[]{:S(2)}) collective-permute-start(f32[80,256]{1,0:T(8,128)S(1)} %get-tuple-element.56), channel_id=1, source_target_pairs={{1,0},{2,1},{5,4},{6,5},{9,8},{10,9},{13,12},{14,13},{17,16},{18,1... | collective-permute-start | bytes 245768 | tf_op jit(solution)/shard_map/ppermute | solution.py:541
  108.9 5.0 %shard_map.42 = f32[8,4,128,128]{3,2,1,0:T(8,128)} custom-call(f32[8,4,128,128]{3,2,1,0:T(8,128)} %bitcast.34, f32[32,4,32,128]{3,2,1,0:T(8,128)} %bitcast.9.refs_1_.arrived_ref), custom_call_target="tpu_custom_call" | custom-call | bytes 16777216 | tf_op jit(solution)/shard_map/pallas_call | solution.py:219
  113.9 3.6 %shard_map.43 = f32[256,16,128]{2,1,0:T(8,128)} custom-call(s32[5]{0:T(128)S(1)} %copy-done.4, f32[256,16,128]{2,1,0:T(8,128)} %bitcast.45, f32[4096,128]{1,0:T(8,128)S(1)} %bitcast.35, f32[256,256]{1,0:T(8,128)S(1)} %slice_bitcast_fusion.refs_3_, f32[32,8,128]{2,1,0:T(8,128)S(1)} %all-to-all-done.3.refs_4_, ...), custom_call_target="tpu_custom_call", output_to_operand_aliasing={{}: (1, {})} | custom-call | bytes 8388608 | tf_op jit(solution)/shard_map/pallas_call | solution.py:653
  (61 shorter events, 9.0 us)
Async XLA Ops:
  0.0 8.6 %collective-permute-start.2 = (f32[128,256]{1,0:T(8,128)}, f32[128,256]{1,0:T(8,128)S(1)}, u32[]{:S(2)}, u32[]{:S(2)}) collective-permute-start(f32[128,256]{1,0:T(8,128)} %bitcast.36), channel_id=1, source_target_pairs={{0,16},{4,68},{8,24},{12,76},{16,0},{20,84},{24,8},{28,92},{32,48}... | collective-permute-start | bytes 393224 | tf_op jit(solution)/shard_map/ppermute | solution.py:536
  3.7 6.4 %collective-permute-start.1 = (f32[128,256]{1,0:T(8,128)}, f32[128,256]{1,0:T(8,128)S(1)}, u32[]{:S(2)}, u32[]{:S(2)}) collective-permute-start(f32[128,256]{1,0:T(8,128)} %bitcast.37), channel_id=1, source_target_pairs={{0,24},{4,100},{8,0},{12,108},{16,8},{20,116},{24,16},{28,124},{32... | collective-permute-start | bytes 393224 | tf_op jit(solution)/shard_map/ppermute | solution.py:536
  4.5 5.7 %collective-permute-start = (f32[128,256]{1,0:T(8,128)}, f32[128,256]{1,0:T(8,128)S(1)}, u32[]{:S(2)}, u32[]{:S(2)}) collective-permute-start(f32[128,256]{1,0:T(8,128)} %bitcast.38), channel_id=1, source_target_pairs={{0,8},{4,36},{8,16},{12,44},{16,24},{20,52},{24,0},{28,60},{32,40}... | collective-permute-start | bytes 393224 | tf_op jit(solution)/shard_map/ppermute | solution.py:536
  5.2 11.1 %collective-permute-start.10 = (f32[2,64,256]{2,1,0:T(8,128)}, f32[2,64,256]{2,1,0:T(8,128)S(1)}, u32[]{:S(2)}, u32[]{:S(2)}) collective-permute-start(f32[2,64,256]{2,1,0:T(8,128)} %bitcast.39), channel_id=1, source_target_pairs={{0,1},{1,2},{2,3},{3,0},{4,5},{5,6},{6,7},{7,4},{8,9},{9,10},{10,1... | collective-permute-start | bytes 393224 | tf_op jit(solution)/shard_map/ppermute | solution.py:555
  6.4 8.7 %collective-permute-start.12 = (f32[2,64,256]{2,1,0:T(8,128)}, f32[2,64,256]{2,1,0:T(8,128)S(1)}, u32[]{:S(2)}, u32[]{:S(2)}) collective-permute-start(f32[2,64,256]{2,1,0:T(8,128)} %bitcast.40), channel_id=1, source_target_pairs={{0,3},{1,0},{2,1},{3,2},{4,7},{5,4},{6,5},{7,6},{8,11},{9,8},{10,9... | collective-permute-start | bytes 393224 | tf_op jit(solution)/shard_map/ppermute | solution.py:555
  8.6 7.7 %collective-permute-start.11 = (f32[2,64,256]{2,1,0:T(8,128)}, f32[2,64,256]{2,1,0:T(8,128)S(1)}, u32[]{:S(2)}, u32[]{:S(2)}) collective-permute-start(f32[2,64,256]{2,1,0:T(8,128)} %bitcast.42), channel_id=1, source_target_pairs={{0,2},{1,3},{2,0},{3,1},{4,6},{5,7},{6,4},{7,5},{8,10},{9,11},{10,... | collective-permute-start | bytes 393224 | tf_op jit(solution)/shard_map/ppermute | solution.py:555
  11.2 16.9 %collective-permute-start.3 = (f32[512,256]{1,0:T(8,128)S(1)}, f32[512,256]{1,0:T(8,128)S(1)}, u32[]{:S(2)}, u32[]{:S(2)}) collective-permute-start(f32[512,256]{1,0:T(8,128)S(1)} %pad_maximum_fusion.refs_2_), channel_id=1, source_target_pairs={{0,32},{4,12},{8,40},{12,20},{16,48},{20,28},{24,56},{28,4},{32,64... | collective-permute-start | bytes 1572872 | tf_op jit(solution)/shard_map/ppermute | solution.py:536
  12.9 15.2 %collective-permute-start.4 = (f32[512,256]{1,0:T(8,128)S(1)}, f32[512,256]{1,0:T(8,128)S(1)}, u32[]{:S(2)}, u32[]{:S(2)}) collective-permute-start(f32[512,256]{1,0:T(8,128)S(1)} %pad_maximum_fusion.refs_2_), channel_id=1, source_target_pairs={{0,96},{4,28},{8,104},{12,4},{16,112},{20,12},{24,120},{28,20},{32... | collective-permute-start | bytes 1572872 | tf_op jit(solution)/shard_map/ppermute | solution.py:536
  15.1 13.6 %collective-permute-start.5 = (f32[512,256]{1,0:T(8,128)S(1)}, f32[512,256]{1,0:T(8,128)S(1)}, u32[]{:S(2)}, u32[]{:S(2)}) collective-permute-start(f32[512,256]{1,0:T(8,128)S(1)} %pad_maximum_fusion.refs_2_), channel_id=1, source_target_pairs={{0,64},{4,20},{8,72},{12,28},{16,80},{20,4},{24,88},{28,12},{32,96... | collective-permute-start | bytes 1572872 | tf_op jit(solution)/shard_map/ppermute | solution.py:536
  17.1 17.6 %all-to-all-start.1 = ((f32[16,48,128]{2,1,0:T(8,128)}), f32[16,48,128]{2,1,0:T(8,128)S(1)}, u32[]{:S(2)}, u32[]{:S(2)}) async-start(f32[16,48,128]{2,1,0:T(8,128)} %broadcast_in_dim.8), calls=%async_computation.1 | async-start | bytes 786432 | tf_op jit(solution)/shard_map/all_to_all | solution.py:566
  28.1 16.1 %copy-start.6 = (f32[512,256]{1,0:T(8,128)}, f32[512,256]{1,0:T(8,128)S(1)}, u32[]{:S(2)}) copy-start(f32[512,256]{1,0:T(8,128)S(1)} %collective-permute-done.4.refs_4_) | copy-start | bytes 1572868
  28.7 15.9 %copy-start.7 = (f32[512,256]{1,0:T(8,128)}, f32[512,256]{1,0:T(8,128)S(1)}, u32[]{:S(2)}) copy-start(f32[512,256]{1,0:T(8,128)S(1)} %collective-permute-done.5.refs_5_) | copy-start | bytes 1572868
  34.7 15.1 %copy-start.1 = (f32[2,8,1,1,8,256]{5,4,3,2,1,0:T(8,128)S(1)}, f32[2,8,1,1,8,256]{5,4,3,2,1,0:T(8,128)}, u32[]{:S(2)}) copy-start(f32[2,8,1,1,8,256]{5,4,3,2,1,0:T(8,128)} %param.4) | copy-start | bytes 393220
  34.7 15.1 %copy-start.3 = (s32[5]{0:T(128)S(1)}, s32[5]{0:T(128)}, u32[]{:S(2)}) copy-start(s32[5]{0:T(128)} %stack.47.refs_0_) | copy-start | bytes 64
  34.7 38.8 %all-to-all-start = ((f32[128,32,128]{2,1,0:T(8,128)}), f32[128,32,128]{2,1,0:T(8,128)}, u32[]{:S(2)}, u32[]{:S(2)}) async-start(f32[128,32,128]{2,1,0:T(8,128)} %bitcast.46), calls=%async_computation | async-start | bytes 4194304 | tf_op jit(solution)/shard_map/all_to_all | solution.py:593
  42.9 5.6 %collective-permute-start.6 = (f32[512,256]{1,0:T(8,128)S(1)}, f32[512,256]{1,0:T(8,128)S(1)}, u32[]{:S(2)}, u32[]{:S(2)}) collective-permute-start(f32[512,256]{1,0:T(8,128)S(1)} %pad_maximum_fusion.refs_2_), channel_id=1, source_target_pairs={{0,4},{4,0},{8,12},{12,8},{16,20},{20,16},{24,28},{28,24},{32,36},... | collective-permute-start | bytes 1572872 | tf_op jit(solution)/shard_map/ppermute | solution.py:596
  44.1 4.4 %collective-permute-start.7 = (f32[512,256]{1,0:T(8,128)S(1)}, f32[512,256]{1,0:T(8,128)S(1)}, u32[]{:S(2)}, u32[]{:S(2)}) collective-permute-start(f32[512,256]{1,0:T(8,128)S(1)} %collective-permute-done.3.refs_3_), channel_id=1, source_target_pairs={{0,4},{4,0},{8,12},{12,8},{16,20},{20,16},{24,28},{28,24},{32,36},... | collective-permute-start | bytes 1572872 | tf_op jit(solution)/shard_map/ppermute | solution.py:596
  44.2 4.3 %collective-permute-start.8 = (f32[512,256]{1,0:T(8,128)S(1)}, f32[512,256]{1,0:T(8,128)S(1)}, u32[]{:S(2)}, u32[]{:S(2)}) collective-permute-start(f32[512,256]{1,0:T(8,128)S(1)} %collective-permute-done.4.refs_4_), channel_id=1, source_target_pairs={{0,4},{4,0},{8,12},{12,8},{16,20},{20,16},{24,28},{28,24},{32,36},... | collective-permute-start | bytes 1572872 | tf_op jit(solution)/shard_map/ppermute | solution.py:596
  44.6 3.9 %collective-permute-start.9 = (f32[512,256]{1,0:T(8,128)S(1)}, f32[512,256]{1,0:T(8,128)S(1)}, u32[]{:S(2)}, u32[]{:S(2)}) collective-permute-start(f32[512,256]{1,0:T(8,128)S(1)} %collective-permute-done.5.refs_5_), channel_id=1, source_target_pairs={{0,4},{4,0},{8,12},{12,8},{16,20},{20,16},{24,28},{28,24},{32,36},... | collective-permute-start | bytes 1572872 | tf_op jit(solution)/shard_map/ppermute | solution.py:596
  44.7 3.7 %collective-permute-start.13 = (f32[16,48,128]{2,1,0:T(8,128)S(1)}, f32[16,48,128]{2,1,0:T(8,128)S(1)}, u32[]{:S(2)}, u32[]{:S(2)}) collective-permute-start(f32[16,48,128]{2,1,0:T(8,128)S(1)} %all-to-all-done.1.refs_15_), channel_id=1, source_target_pairs={{0,4},{4,0},{8,12},{12,8},{16,20},{20,16},{24,28},{28,24},{32,36},... | collective-permute-start | bytes 1179656 | tf_op jit(solution)/shard_map/ppermute | solution.py:597
  48.5 1.3 %copy-start.11 = (f32[512,256]{1,0:T(8,128)}, f32[512,256]{1,0:T(8,128)S(1)}, u32[]{:S(2)}) copy-start(f32[512,256]{1,0:T(8,128)S(1)} %collective-permute-done.9.refs_9_) | copy-start | bytes 1572868
  66.0 1.9 %collective-permute-start.17 = (f32[16,64,128]{2,1,0:T(8,128)S(1)}, f32[16,64,128]{2,1,0:T(8,128)S(1)}, u32[]{:S(2)}, u32[]{:S(2)}) collective-permute-start(f32[16,64,128]{2,1,0:T(8,128)S(1)} %get-tuple-element.47), channel_id=1, source_target_pairs={{0,4},{4,0},{8,12},{12,8},{16,20},{20,16},{24,28},{28,24},{32,36},... | collective-permute-start | bytes 1572872 | tf_op jit(solution)/shard_map/ppermute | solution.py:617
  73.5 14.2 %all-to-all-start.2 = ((f32[16,64,128]{2,1,0:T(8,128)}), f32[16,64,128]{2,1,0:T(8,128)S(1)}, u32[]{:S(2)}, u32[]{:S(2)}) async-start(f32[16,64,128]{2,1,0:T(8,128)} %add.13), calls=%async_computation.2 | async-start | bytes 1048576 | tf_op jit(solution)/shard_map/all_to_all | solution.py:566
  77.3 10.5 %copy-start.4 = (s32[5]{0:T(128)S(1)}, s32[5]{0:T(128)}, u32[]{:S(2)}) copy-start(s32[5]{0:T(128)} %stack.47.refs_0_) | copy-start | bytes 64
  83.8 9.2 %collective-permute-start.14 = (f32[64,512]{1,0:T(8,128)}, f32[64,512]{1,0:T(8,128)S(1)}, u32[]{:S(2)}, u32[]{:S(2)}) collective-permute-start(f32[64,512]{1,0:T(8,128)} %get-tuple-element.43), channel_id=1, source_target_pairs={{0,1},{1,2},{2,3},{3,0},{4,5},{5,6},{6,7},{7,4},{8,9},{9,10},{10,1... | collective-permute-start | bytes 393224 | tf_op jit(solution)/shard_map/ppermute | solution.py:636
  84.2 8.8 %collective-permute-start.15 = (f32[64,512]{1,0:T(8,128)}, f32[64,512]{1,0:T(8,128)S(1)}, u32[]{:S(2)}, u32[]{:S(2)}) collective-permute-start(f32[64,512]{1,0:T(8,128)} %get-tuple-element.44), channel_id=1, source_target_pairs={{0,2},{1,3},{2,0},{3,1},{4,6},{5,7},{6,4},{7,5},{8,10},{9,11},{10,... | collective-permute-start | bytes 393224 | tf_op jit(solution)/shard_map/ppermute | solution.py:636
  85.6 7.7 %collective-permute-start.16 = (f32[64,512]{1,0:T(8,128)}, f32[64,512]{1,0:T(8,128)S(1)}, u32[]{:S(2)}, u32[]{:S(2)}) collective-permute-start(f32[64,512]{1,0:T(8,128)} %get-tuple-element.45), channel_id=1, source_target_pairs={{0,3},{1,0},{2,1},{3,2},{4,7},{5,4},{6,5},{7,6},{8,11},{9,8},{10,9... | collective-permute-start | bytes 393224 | tf_op jit(solution)/shard_map/ppermute | solution.py:636
  95.8 18.1 %all-to-all-start.3 = ((f32[32,8,128]{2,1,0:T(8,128)}), f32[32,8,128]{2,1,0:T(8,128)S(1)}, u32[]{:S(2)}, u32[]{:S(2)}) async-start(f32[32,8,128]{2,1,0:T(8,128)} %get-tuple-element.52), calls=%async_computation.3 | async-start | bytes 262144 | tf_op jit(solution)/shard_map/all_to_all | solution.py:649
  104.1 9.8 %collective-permute-start.18 = (f32[80,256]{1,0:T(8,128)S(1)}, f32[80,256]{1,0:T(8,128)S(1)}, u32[]{:S(2)}, u32[]{:S(2)}) collective-permute-start(f32[80,256]{1,0:T(8,128)S(1)} %get-tuple-element.54), channel_id=1, source_target_pairs={{3,0},{0,1},{7,4},{4,5},{11,8},{8,9},{15,12},{12,13},{19,16},{16,1... | collective-permute-start | bytes 245768 | tf_op jit(solution)/shard_map/ppermute | solution.py:541
  106.2 7.6 %collective-permute-start.19 = (f32[80,256]{1,0:T(8,128)S(1)}, f32[80,256]{1,0:T(8,128)S(1)}, u32[]{:S(2)}, u32[]{:S(2)}) collective-permute-start(f32[80,256]{1,0:T(8,128)S(1)} %get-tuple-element.55), channel_id=1, source_target_pairs={{2,0},{3,1},{6,4},{7,5},{10,8},{11,9},{14,12},{15,13},{18,16},{19,... | collective-permute-start | bytes 245768 | tf_op jit(solution)/shard_map/ppermute | solution.py:541
  107.5 6.3 %collective-permute-start.20 = (f32[80,256]{1,0:T(8,128)S(1)}, f32[80,256]{1,0:T(8,128)S(1)}, u32[]{:S(2)}, u32[]{:S(2)}) collective-permute-start(f32[80,256]{1,0:T(8,128)S(1)} %get-tuple-element.56), channel_id=1, source_target_pairs={{1,0},{2,1},{5,4},{6,5},{9,8},{10,9},{13,12},{14,13},{17,16},{18,1... | collective-permute-start | bytes 245768 | tf_op jit(solution)/shard_map/ppermute | solution.py:541
  108.8 5.1 %copy-start = (f32[32,1,8,8,1,256]{5,4,3,2,1,0:T(1,128)S(1)}, f32[32,1,8,8,1,256]{5,4,3,2,1,0:T(1,128)}, u32[]{:S(2)}) copy-start(f32[32,1,8,8,1,256]{5,4,3,2,1,0:T(1,128)} %param.3) | copy-start | bytes 6291460
  (5 other events, 4.6 us)

commit v2 on v1

--- a/solution.py
+++ b/solution.py
@@ -365,24 +365,16 @@
 
 
 def image_body(
-    place_ref, staged, wait, made, flush, arrived_ref, both_ref, strips_ref, in_sem
+    place_ref, staged, wait, made, flush, both_ref, strips_ref
 ):
     source_ref, rest_ref, high_ref, low_ref = staged
     chunk_refs = made
     col_place = place_ref[4]
-    arriving = [
-        pltpu.make_async_copy(source_ref.at[:, col], arrived_ref.at[col], in_sem.at[col])
-        for col in range(N_COL)
-    ]
-    for copy in arriving:
-        copy.start()
-    wait(None)
     for col in range(N_COL):
-        arriving[col].wait()
 
         def turn(low, carry):
             for half in range(2):
-                tiles = mirror_tiles(arrived_ref.at[col], low, half)
+                tiles = mirror_tiles(source_ref.at[:, col], low, half)
                 for (high, group), tile in tiles.items():
                     inner = 4 * high + low
                     if group == 0 and col < 2:
@@ -622,13 +614,11 @@
         [shape(STRIP, 2 * BLK)] * 4,
         image_ins,
         scratch=[
-            pltpu.VMEM((N_COL, N_ROW, 32, 128), F32),
             wide_shape,
             pltpu.VMEM((ROWS, 2 * BLK), F32),
-            pltpu.SemaphoreType.DMA((N_COL,)),
         ],
-        raw_in=(0,),
-        eager=False,
+        near=(0,),
+        limit=VMEM_LIMIT,
         flops=2**32,
         size=2**24,
     )(place, *image_ins)

time: 119 us -> 119 us (level)
  no operation moved by 1% of the time
where the time goes in v2:
time: 119 us; the launch traced here: 118 us
  starting transfers between devices  50.3 us (42%)
  Pallas kernels  38 us (32%)
  waiting for transfers between devices  21.2 us (18%)
  local copies, waits for them, and re-layouts  6.1 us (5%)
  other arithmetic  1.88 us (2%)
    pallas_call x1, Pallas kernels, on_device(): call(direct_body, [shape(2, BLK, BLK), split_shape, split_shape, shape(N_...  15.4 us
    ppermute x6, starting transfers between devices, around(): lax.ppermute(piece, 'row', ring(first, d))  10.3 us
    all_to_all x2, starting transfers between devices, exchange(): lax.all_to_all(value, 'row', split_axis=0, concat_axis=0, tiled=True, axi...  8.94 us
    all_to_all x1, starting transfers between devices, on_device(): lax.all_to_all(across, 'row', split_axis=0, concat_axis=0, tiled=True)  8.29 us
    all_to_all x1, starting transfers between devices, on_device(): lax.all_to_all(outgoing.reshape(N_ROW * N_COL, 32, 128), ('row', 'col'),...  8.15 us
    pallas_call x1, Pallas kernels, on_device(): call(image_body, [shape(STRIP, 2 * BLK)] * 4, image_ins, scratch=[wide_sh...  6.68 us
    all_to_all x2, waiting for transfers between devices, exchange(): lax.all_to_all(value, 'row', split_axis=0, concat_axis=0, tiled=True, axi...  6.01 us
    pallas_call x1, Pallas kernels, on_device(): call(pack_body, [part_shape, wide], [high_shape], scratch=[pltpu.VMEM(hig...  5.12 us
  transfers between devices with their start and end apart: 25, of which 7 were waited for; matrix products, arithmetic and copies ran while one was open for 4% of the time, Pallas kernels for 28%

profile of v2, /device:TPU:1, one launch (start us, length us, event | category | flops | bytes accessed | tf_op | source)
XLA Modules:
  0.0 117.8 jit_solution(3796708751172262719)
XLA Ops:
  0.0 3.7 %collective-permute-start.2 = (f32[128,256]{1,0:T(8,128)}, f32[128,256]{1,0:T(8,128)S(1)}, u32[]{:S(2)}, u32[]{:S(2)}) collective-permute-start(f32[128,256]{1,0:T(8,128)} %bitcast.36), channel_id=1, source_target_pairs={{0,16},{4,68},{8,24},{12,76},{16,0},{20,84},{24,8},{28,92},{32,48}... | collective-permute-start | bytes 393224 | tf_op jit(solution)/shard_map/ppermute | solution.py:528
  5.2 1.2 %collective-permute-start.10 = (f32[2,64,256]{2,1,0:T(8,128)}, f32[2,64,256]{2,1,0:T(8,128)S(1)}, u32[]{:S(2)}, u32[]{:S(2)}) collective-permute-start(f32[2,64,256]{2,1,0:T(8,128)} %bitcast.39), channel_id=1, source_target_pairs={{0,1},{1,2},{2,3},{3,0},{4,5},{5,6},{6,7},{7,4},{8,9},{9,10},{10,1... | collective-permute-start | bytes 393224 | tf_op jit(solution)/shard_map/ppermute | solution.py:547
  6.4 1.5 %collective-permute-start.12 = (f32[2,64,256]{2,1,0:T(8,128)}, f32[2,64,256]{2,1,0:T(8,128)S(1)}, u32[]{:S(2)}, u32[]{:S(2)}) collective-permute-start(f32[2,64,256]{2,1,0:T(8,128)} %bitcast.40), channel_id=1, source_target_pairs={{0,3},{1,0},{2,1},{3,2},{4,7},{5,4},{6,5},{7,6},{8,11},{9,8},{10,9... | collective-permute-start | bytes 393224 | tf_op jit(solution)/shard_map/ppermute | solution.py:547
  8.6 1.5 %collective-permute-start.11 = (f32[2,64,256]{2,1,0:T(8,128)}, f32[2,64,256]{2,1,0:T(8,128)S(1)}, u32[]{:S(2)}, u32[]{:S(2)}) collective-permute-start(f32[2,64,256]{2,1,0:T(8,128)} %bitcast.42), channel_id=1, source_target_pairs={{0,2},{1,3},{2,0},{3,1},{4,6},{5,7},{6,4},{7,5},{8,10},{9,11},{10,... | collective-permute-start | bytes 393224 | tf_op jit(solution)/shard_map/ppermute | solution.py:547
  10.2 1.0 pad_maximum_fusion.refs_2_
  11.2 1.7 %collective-permute-start.3 = (f32[512,256]{1,0:T(8,128)S(1)}, f32[512,256]{1,0:T(8,128)S(1)}, u32[]{:S(2)}, u32[]{:S(2)}) collective-permute-start(f32[512,256]{1,0:T(8,128)S(1)} %pad_maximum_fusion.refs_2_), channel_id=1, source_target_pairs={{0,32},{4,12},{8,40},{12,20},{16,48},{20,28},{24,56},{28,4},{32,64... | collective-permute-start | bytes 1572872 | tf_op jit(solution)/shard_map/ppermute | solution.py:528
  12.9 2.2 %collective-permute-start.4 = (f32[512,256]{1,0:T(8,128)S(1)}, f32[512,256]{1,0:T(8,128)S(1)}, u32[]{:S(2)}, u32[]{:S(2)}) collective-permute-start(f32[512,256]{1,0:T(8,128)S(1)} %pad_maximum_fusion.refs_2_), channel_id=1, source_target_pairs={{0,96},{4,28},{8,104},{12,4},{16,112},{20,12},{24,120},{28,20},{32... | collective-permute-start | bytes 1572872 | tf_op jit(solution)/shard_map/ppermute | solution.py:528
  15.1 1.2 %collective-permute-start.5 = (f32[512,256]{1,0:T(8,128)S(1)}, f32[512,256]{1,0:T(8,128)S(1)}, u32[]{:S(2)}, u32[]{:S(2)}) collective-permute-start(f32[512,256]{1,0:T(8,128)S(1)} %pad_maximum_fusion.refs_2_), channel_id=1, source_target_pairs={{0,64},{4,20},{8,72},{12,28},{16,80},{20,4},{24,88},{28,12},{32,96... | collective-permute-start | bytes 1572872 | tf_op jit(solution)/shard_map/ppermute | solution.py:528
  17.1 5.2 %all-to-all-start.1 = ((f32[16,48,128]{2,1,0:T(8,128)}), f32[16,48,128]{2,1,0:T(8,128)S(1)}, u32[]{:S(2)}, u32[]{:S(2)}) async-start(f32[16,48,128]{2,1,0:T(8,128)} %broadcast_in_dim.8), calls=%async_computation.1 | async-start | bytes 786432 | tf_op jit(solution)/shard_map/all_to_all | solution.py:558
  22.9 5.1 %shard_map.37 = (f32[4,1024,128]{2,1,0:T(8,128)}, f32[8,256,256]{2,1,0:T(8,128)}) custom-call(s32[5]{0:T(128)} %stack.47.refs_0_, f32[2,2048,128]{2,1,0:T(8,128)} %bitcast.33), custom_call_target="tpu_custom_call" | custom-call | bytes 16777216 | tf_op jit(solution)/shard_map/pallas_call | solution.py:569
  28.7 6.0 %all-to-all-done.1.refs_15_ = f32[16,48,128]{2,1,0:T(8,128)S(1)} async-done(((f32[16,48,128]{2,1,0:T(8,128)}), f32[16,48,128]{2,1,0:T(8,128)S(1)}, u32[]{:S(2)}, u32[]{:S(2)}) %all-to-all-start.1) | async-done | bytes 393248 | tf_op jit(solution)/shard_map/all_to_all | solution.py:558
  34.7 8.1 %all-to-all-start = ((f32[128,32,128]{2,1,0:T(8,128)}), f32[128,32,128]{2,1,0:T(8,128)}, u32[]{:S(2)}, u32[]{:S(2)}) async-start(f32[128,32,128]{2,1,0:T(8,128)} %bitcast.46), calls=%async_computation | async-start | bytes 4194304 | tf_op jit(solution)/shard_map/all_to_all | solution.py:585
  42.9 1.2 %collective-permute-start.6 = (f32[512,256]{1,0:T(8,128)S(1)}, f32[512,256]{1,0:T(8,128)S(1)}, u32[]{:S(2)}, u32[]{:S(2)}) collective-permute-start(f32[512,256]{1,0:T(8,128)S(1)} %pad_maximum_fusion.refs_2_), channel_id=1, source_target_pairs={{0,4},{4,0},{8,12},{12,8},{16,20},{20,16},{24,28},{28,24},{32,36},... | collective-permute-start | bytes 1572872 | tf_op jit(solution)/shard_map/ppermute | solution.py:588
  45.1 3.3 %collective-permute-done.13.refs_16_ = f32[16,48,128]{2,1,0:T(8,128)S(1)} collective-permute-done((f32[16,48,128]{2,1,0:T(8,128)S(1)}, f32[16,48,128]{2,1,0:T(8,128)S(1)}, u32[]{:S(2)}, u32[]{:S(2)}) %collective-permute-start.13) | collective-permute-done | bytes 393248 | tf_op jit(solution)/shard_map/ppermute | solution.py:589
  49.8 15.4 %shard_map.38 = (f32[2,256,256]{2,1,0:T(8,128)S(1)}, bf16[8,256,512]{2,1,0:T(8,128)(2,1)}, bf16[8,256,512]{2,1,0:T(8,128)(2,1)}, f32[16,64,128]{2,1,0:T(8,128)S(1)}, f32[16,64,128]{2,1,0:T(8,128)S(1)}) custom-call(s32[5]{0:T(128)S(1)} %copy-done.3, f32[8,256,256]{2,1,0:T(8,128)} %get-tuple-element.34.refs_1_, f32[512,256]{1,0:T(8,128)S(1)} %pad_maximum_fusion.refs_2_, ...), custom_call_target="tpu_custom_call" | custom-call | flops 8589934592 | bytes 16777216 | tf_op jit(solution)/shard_map/pallas_call | solution.py:596
  66.3 1.5 %collective-permute-done.17 = f32[16,64,128]{2,1,0:T(8,128)S(1)} collective-permute-done((f32[16,64,128]{2,1,0:T(8,128)S(1)}, f32[16,64,128]{2,1,0:T(8,128)S(1)}, u32[]{:S(2)}, u32[]{:S(2)}) %collective-permute-start.17) | collective-permute-done | bytes 524320 | tf_op jit(solution)/shard_map/ppermute | solution.py:609
  67.9 0.9 add.13
  68.8 4.8 %all-to-all-done = f32[128,32,128]{2,1,0:T(8,128)} async-done(((f32[128,32,128]{2,1,0:T(8,128)}), f32[128,32,128]{2,1,0:T(8,128)}, u32[]{:S(2)}, u32[]{:S(2)}) %all-to-all-start) | async-done | bytes 2097184 | tf_op jit(solution)/shard_map/all_to_all | solution.py:585
  73.5 3.8 %all-to-all-start.2 = ((f32[16,64,128]{2,1,0:T(8,128)}), f32[16,64,128]{2,1,0:T(8,128)S(1)}, u32[]{:S(2)}, u32[]{:S(2)}) async-start(f32[16,64,128]{2,1,0:T(8,128)} %add.13), calls=%async_computation.2 | async-start | bytes 1048576 | tf_op jit(solution)/shard_map/all_to_all | solution.py:558
  77.3 6.7 %shard_map.39 = (f32[64,512]{1,0:T(8,128)}, f32[64,512]{1,0:T(8,128)}, f32[64,512]{1,0:T(8,128)}, f32[64,512]{1,0:T(8,128)}) custom-call(s32[5]{0:T(128)} %stack.47.refs_0_, f32[32,4,32,128]{3,2,1,0:T(8,128)} %bitcast.9.refs_1_.arrived_ref, f32[2,256,256]{2,1,0:T(8,128)} %copy-done.5, bf16[8,256,512]{2,1,0:T(8,128)(2,1)} %get-tuple-element.40.refs_3_, ...), custom_call_target="tpu_custom_call" | custom-call | flops 4294967296 | bytes 16777216 | tf_op jit(solution)/shard_map/pallas_call | solution.py:612
  84.4 1.4 %collective-permute-start.15 = (f32[64,512]{1,0:T(8,128)}, f32[64,512]{1,0:T(8,128)S(1)}, u32[]{:S(2)}, u32[]{:S(2)}) collective-permute-start(f32[64,512]{1,0:T(8,128)} %get-tuple-element.44), channel_id=1, source_target_pairs={{0,2},{1,3},{2,0},{3,1},{4,6},{5,7},{6,4},{7,5},{8,10},{9,11},{10,... | collective-permute-start | bytes 393224 | tf_op jit(solution)/shard_map/ppermute | solution.py:626
  85.8 1.2 collective-permute-start.16
  87.0 1.0 slice_bitcast_fusion.refs_3_
  88.6 4.6 %collective-permute-done.14.refs_2_ = f32[64,512]{1,0:T(8,128)S(1)} collective-permute-done((f32[64,512]{1,0:T(8,128)}, f32[64,512]{1,0:T(8,128)S(1)}, u32[]{:S(2)}, u32[]{:S(2)}) %collective-permute-start.14) | collective-permute-done | bytes 131104 | tf_op jit(solution)/shard_map/ppermute | solution.py:626
  93.5 0.9 copy-done.2
  94.4 1.6 %shard_map.41 = (f32[32,8,128]{2,1,0:T(8,128)}, f32[80,256]{1,0:T(8,128)S(1)}, f32[80,256]{1,0:T(8,128)S(1)}, f32[80,256]{1,0:T(8,128)S(1)}, f32[80,256]{1,0:T(8,128)S(1)}) custom-call(s32[5]{0:T(128)S(1)} %copy-done.4, f32[64,512]{1,0:T(8,128)S(1)} %copy-done.2, f32[64,512]{1,0:T(8,128)S(1)} %collective-permute-done.14.refs_2_, ...), custom_call_target="tpu_custom_call" | custom-call | bytes 2097152 | tf_op jit(solution)/shard_map/pallas_call | solution.py:631
  96.0 8.3 %all-to-all-start.3 = ((f32[32,8,128]{2,1,0:T(8,128)}), f32[32,8,128]{2,1,0:T(8,128)S(1)}, u32[]{:S(2)}, u32[]{:S(2)}) async-start(f32[32,8,128]{2,1,0:T(8,128)} %get-tuple-element.52), calls=%async_computation.3 | async-start | bytes 262144 | tf_op jit(solution)/shard_map/all_to_all | solution.py:639
  104.3 2.2 %collective-permute-start.18 = (f32[80,256]{1,0:T(8,128)S(1)}, f32[80,256]{1,0:T(8,128)S(1)}, u32[]{:S(2)}, u32[]{:S(2)}) collective-permute-start(f32[80,256]{1,0:T(8,128)S(1)} %get-tuple-element.54), channel_id=1, source_target_pairs={{3,0},{0,1},{7,4},{4,5},{11,8},{8,9},{15,12},{12,13},{19,16},{16,1... | collective-permute-start | bytes 245768 | tf_op jit(solution)/shard_map/ppermute | solution.py:533
  106.4 1.3 %collective-permute-start.19 = (f32[80,256]{1,0:T(8,128)S(1)}, f32[80,256]{1,0:T(8,128)S(1)}, u32[]{:S(2)}, u32[]{:S(2)}) collective-permute-start(f32[80,256]{1,0:T(8,128)S(1)} %get-tuple-element.55), channel_id=1, source_target_pairs={{2,0},{3,1},{6,4},{7,5},{10,8},{11,9},{14,12},{15,13},{18,16},{19,... | collective-permute-start | bytes 245768 | tf_op jit(solution)/shard_map/ppermute | solution.py:533
  107.7 1.3 %collective-permute-start.20 = (f32[80,256]{1,0:T(8,128)S(1)}, f32[80,256]{1,0:T(8,128)S(1)}, u32[]{:S(2)}, u32[]{:S(2)}) collective-permute-start(f32[80,256]{1,0:T(8,128)S(1)} %get-tuple-element.56), channel_id=1, source_target_pairs={{1,0},{2,1},{5,4},{6,5},{9,8},{10,9},{13,12},{14,13},{17,16},{18,1... | collective-permute-start | bytes 245768 | tf_op jit(solution)/shard_map/ppermute | solution.py:533
  109.0 5.0 %shard_map.42 = f32[8,4,128,128]{3,2,1,0:T(8,128)} custom-call(f32[8,4,128,128]{3,2,1,0:T(8,128)} %bitcast.34, f32[32,4,32,128]{3,2,1,0:T(8,128)} %bitcast.9.refs_1_.arrived_ref), custom_call_target="tpu_custom_call" | custom-call | bytes 16777216 | tf_op jit(solution)/shard_map/pallas_call | solution.py:219
  114.1 3.6 %shard_map.43 = f32[256,16,128]{2,1,0:T(8,128)} custom-call(s32[5]{0:T(128)S(1)} %copy-done.4, f32[256,16,128]{2,1,0:T(8,128)} %bitcast.45, f32[4096,128]{1,0:T(8,128)S(1)} %bitcast.35, f32[256,256]{1,0:T(8,128)S(1)} %slice_bitcast_fusion.refs_3_, f32[32,8,128]{2,1,0:T(8,128)S(1)} %all-to-all-done.3.refs_4_, ...), custom_call_target="tpu_custom_call", output_to_operand_aliasing={{}: (1, {})} | custom-call | bytes 8388608 | tf_op jit(solution)/shard_map/pallas_call | solution.py:643
  (61 shorter events, 9.0 us)
Async XLA Ops:
  0.0 8.6 %collective-permute-start.2 = (f32[128,256]{1,0:T(8,128)}, f32[128,256]{1,0:T(8,128)S(1)}, u32[]{:S(2)}, u32[]{:S(2)}) collective-permute-start(f32[128,256]{1,0:T(8,128)} %bitcast.36), channel_id=1, source_target_pairs={{0,16},{4,68},{8,24},{12,76},{16,0},{20,84},{24,8},{28,92},{32,48}... | collective-permute-start | bytes 393224 | tf_op jit(solution)/shard_map/ppermute | solution.py:528
  3.7 6.4 %collective-permute-start.1 = (f32[128,256]{1,0:T(8,128)}, f32[128,256]{1,0:T(8,128)S(1)}, u32[]{:S(2)}, u32[]{:S(2)}) collective-permute-start(f32[128,256]{1,0:T(8,128)} %bitcast.37), channel_id=1, source_target_pairs={{0,24},{4,100},{8,0},{12,108},{16,8},{20,116},{24,16},{28,124},{32... | collective-permute-start | bytes 393224 | tf_op jit(solution)/shard_map/ppermute | solution.py:528
  4.5 5.7 %collective-permute-start = (f32[128,256]{1,0:T(8,128)}, f32[128,256]{1,0:T(8,128)S(1)}, u32[]{:S(2)}, u32[]{:S(2)}) collective-permute-start(f32[128,256]{1,0:T(8,128)} %bitcast.38), channel_id=1, source_target_pairs={{0,8},{4,36},{8,16},{12,44},{16,24},{20,52},{24,0},{28,60},{32,40}... | collective-permute-start | bytes 393224 | tf_op jit(solution)/shard_map/ppermute | solution.py:528
  5.2 11.1 %collective-permute-start.10 = (f32[2,64,256]{2,1,0:T(8,128)}, f32[2,64,256]{2,1,0:T(8,128)S(1)}, u32[]{:S(2)}, u32[]{:S(2)}) collective-permute-start(f32[2,64,256]{2,1,0:T(8,128)} %bitcast.39), channel_id=1, source_target_pairs={{0,1},{1,2},{2,3},{3,0},{4,5},{5,6},{6,7},{7,4},{8,9},{9,10},{10,1... | collective-permute-start | bytes 393224 | tf_op jit(solution)/shard_map/ppermute | solution.py:547
  6.4 8.7 %collective-permute-start.12 = (f32[2,64,256]{2,1,0:T(8,128)}, f32[2,64,256]{2,1,0:T(8,128)S(1)}, u32[]{:S(2)}, u32[]{:S(2)}) collective-permute-start(f32[2,64,256]{2,1,0:T(8,128)} %bitcast.40), channel_id=1, source_target_pairs={{0,3},{1,0},{2,1},{3,2},{4,7},{5,4},{6,5},{7,6},{8,11},{9,8},{10,9... | collective-permute-start | bytes 393224 | tf_op jit(solution)/shard_map/ppermute | solution.py:547
  8.6 7.7 %collective-permute-start.11 = (f32[2,64,256]{2,1,0:T(8,128)}, f32[2,64,256]{2,1,0:T(8,128)S(1)}, u32[]{:S(2)}, u32[]{:S(2)}) collective-permute-start(f32[2,64,256]{2,1,0:T(8,128)} %bitcast.42), channel_id=1, source_target_pairs={{0,2},{1,3},{2,0},{3,1},{4,6},{5,7},{6,4},{7,5},{8,10},{9,11},{10,... | collective-permute-start | bytes 393224 | tf_op jit(solution)/shard_map/ppermute | solution.py:547
  11.2 16.9 %collective-permute-start.3 = (f32[512,256]{1,0:T(8,128)S(1)}, f32[512,256]{1,0:T(8,128)S(1)}, u32[]{:S(2)}, u32[]{:S(2)}) collective-permute-start(f32[512,256]{1,0:T(8,128)S(1)} %pad_maximum_fusion.refs_2_), channel_id=1, source_target_pairs={{0,32},{4,12},{8,40},{12,20},{16,48},{20,28},{24,56},{28,4},{32,64... | collective-permute-start | bytes 1572872 | tf_op jit(solution)/shard_map/ppermute | solution.py:528
  12.9 15.2 %collective-permute-start.4 = (f32[512,256]{1,0:T(8,128)S(1)}, f32[512,256]{1,0:T(8,128)S(1)}, u32[]{:S(2)}, u32[]{:S(2)}) collective-permute-start(f32[512,256]{1,0:T(8,128)S(1)} %pad_maximum_fusion.refs_2_), channel_id=1, source_target_pairs={{0,96},{4,28},{8,104},{12,4},{16,112},{20,12},{24,120},{28,20},{32... | collective-permute-start | bytes 1572872 | tf_op jit(solution)/shard_map/ppermute | solution.py:528
  15.1 13.6 %collective-permute-start.5 = (f32[512,256]{1,0:T(8,128)S(1)}, f32[512,256]{1,0:T(8,128)S(1)}, u32[]{:S(2)}, u32[]{:S(2)}) collective-permute-start(f32[512,256]{1,0:T(8,128)S(1)} %pad_maximum_fusion.refs_2_), channel_id=1, source_target_pairs={{0,64},{4,20},{8,72},{12,28},{16,80},{20,4},{24,88},{28,12},{32,96... | collective-permute-start | bytes 1572872 | tf_op jit(solution)/shard_map/ppermute | solution.py:528
  17.1 17.6 %all-to-all-start.1 = ((f32[16,48,128]{2,1,0:T(8,128)}), f32[16,48,128]{2,1,0:T(8,128)S(1)}, u32[]{:S(2)}, u32[]{:S(2)}) async-start(f32[16,48,128]{2,1,0:T(8,128)} %broadcast_in_dim.8), calls=%async_computation.1 | async-start | bytes 786432 | tf_op jit(solution)/shard_map/all_to_all | solution.py:558
  28.1 16.1 %copy-start.6 = (f32[512,256]{1,0:T(8,128)}, f32[512,256]{1,0:T(8,128)S(1)}, u32[]{:S(2)}) copy-start(f32[512,256]{1,0:T(8,128)S(1)} %collective-permute-done.4.refs_4_) | copy-start | bytes 1572868
  28.7 15.9 %copy-start.7 = (f32[512,256]{1,0:T(8,128)}, f32[512,256]{1,0:T(8,128)S(1)}, u32[]{:S(2)}) copy-start(f32[512,256]{1,0:T(8,128)S(1)} %collective-permute-done.5.refs_5_) | copy-start | bytes 1572868
  34.7 15.1 %copy-start.1 = (f32[2,8,1,1,8,256]{5,4,3,2,1,0:T(8,128)S(1)}, f32[2,8,1,1,8,256]{5,4,3,2,1,0:T(8,128)}, u32[]{:S(2)}) copy-start(f32[2,8,1,1,8,256]{5,4,3,2,1,0:T(8,128)} %param.4) | copy-start | bytes 393220
  34.7 15.1 %copy-start.3 = (s32[5]{0:T(128)S(1)}, s32[5]{0:T(128)}, u32[]{:S(2)}) copy-start(s32[5]{0:T(128)} %stack.47.refs_0_) | copy-start | bytes 64
  34.7 38.8 %all-to-all-start = ((f32[128,32,128]{2,1,0:T(8,128)}), f32[128,32,128]{2,1,0:T(8,128)}, u32[]{:S(2)}, u32[]{:S(2)}) async-start(f32[128,32,128]{2,1,0:T(8,128)} %bitcast.46), calls=%async_computation | async-start | bytes 4194304 | tf_op jit(solution)/shard_map/all_to_all | solution.py:585
  42.9 5.6 %collective-permute-start.6 = (f32[512,256]{1,0:T(8,128)S(1)}, f32[512,256]{1,0:T(8,128)S(1)}, u32[]{:S(2)}, u32[]{:S(2)}) collective-permute-start(f32[512,256]{1,0:T(8,128)S(1)} %pad_maximum_fusion.refs_2_), channel_id=1, source_target_pairs={{0,4},{4,0},{8,12},{12,8},{16,20},{20,16},{24,28},{28,24},{32,36},... | collective-permute-start | bytes 1572872 | tf_op jit(solution)/shard_map/ppermute | solution.py:588
  44.1 4.4 %collective-permute-start.7 = (f32[512,256]{1,0:T(8,128)S(1)}, f32[512,256]{1,0:T(8,128)S(1)}, u32[]{:S(2)}, u32[]{:S(2)}) collective-permute-start(f32[512,256]{1,0:T(8,128)S(1)} %collective-permute-done.3.refs_3_), channel_id=1, source_target_pairs={{0,4},{4,0},{8,12},{12,8},{16,20},{20,16},{24,28},{28,24},{32,36},... | collective-permute-start | bytes 1572872 | tf_op jit(solution)/shard_map/ppermute | solution.py:588
  44.2 4.3 %collective-permute-start.8 = (f32[512,256]{1,0:T(8,128)S(1)}, f32[512,256]{1,0:T(8,128)S(1)}, u32[]{:S(2)}, u32[]{:S(2)}) collective-permute-start(f32[512,256]{1,0:T(8,128)S(1)} %collective-permute-done.4.refs_4_), channel_id=1, source_target_pairs={{0,4},{4,0},{8,12},{12,8},{16,20},{20,16},{24,28},{28,24},{32,36},... | collective-permute-start | bytes 1572872 | tf_op jit(solution)/shard_map/ppermute | solution.py:588
  44.6 3.9 %collective-permute-start.9 = (f32[512,256]{1,0:T(8,128)S(1)}, f32[512,256]{1,0:T(8,128)S(1)}, u32[]{:S(2)}, u32[]{:S(2)}) collective-permute-start(f32[512,256]{1,0:T(8,128)S(1)} %collective-permute-done.5.refs_5_), channel_id=1, source_target_pairs={{0,4},{4,0},{8,12},{12,8},{16,20},{20,16},{24,28},{28,24},{32,36},... | collective-permute-start | bytes 1572872 | tf_op jit(solution)/shard_map/ppermute | solution.py:588
  44.7 3.7 %collective-permute-start.13 = (f32[16,48,128]{2,1,0:T(8,128)S(1)}, f32[16,48,128]{2,1,0:T(8,128)S(1)}, u32[]{:S(2)}, u32[]{:S(2)}) collective-permute-start(f32[16,48,128]{2,1,0:T(8,128)S(1)} %all-to-all-done.1.refs_15_), channel_id=1, source_target_pairs={{0,4},{4,0},{8,12},{12,8},{16,20},{20,16},{24,28},{28,24},{32,36},... | collective-permute-start | bytes 1179656 | tf_op jit(solution)/shard_map/ppermute | solution.py:589
  48.5 1.3 %copy-start.11 = (f32[512,256]{1,0:T(8,128)}, f32[512,256]{1,0:T(8,128)S(1)}, u32[]{:S(2)}) copy-start(f32[512,256]{1,0:T(8,128)S(1)} %collective-permute-done.9.refs_9_) | copy-start | bytes 1572868
  66.0 1.9 %collective-permute-start.17 = (f32[16,64,128]{2,1,0:T(8,128)S(1)}, f32[16,64,128]{2,1,0:T(8,128)S(1)}, u32[]{:S(2)}, u32[]{:S(2)}) collective-permute-start(f32[16,64,128]{2,1,0:T(8,128)S(1)} %get-tuple-element.47), channel_id=1, source_target_pairs={{0,4},{4,0},{8,12},{12,8},{16,20},{20,16},{24,28},{28,24},{32,36},... | collective-permute-start | bytes 1572872 | tf_op jit(solution)/shard_map/ppermute | solution.py:609
  73.5 14.4 %all-to-all-start.2 = ((f32[16,64,128]{2,1,0:T(8,128)}), f32[16,64,128]{2,1,0:T(8,128)S(1)}, u32[]{:S(2)}, u32[]{:S(2)}) async-start(f32[16,64,128]{2,1,0:T(8,128)} %add.13), calls=%async_computation.2 | async-start | bytes 1048576 | tf_op jit(solution)/shard_map/all_to_all | solution.py:558
  77.3 10.7 %copy-start.4 = (s32[5]{0:T(128)S(1)}, s32[5]{0:T(128)}, u32[]{:S(2)}) copy-start(s32[5]{0:T(128)} %stack.47.refs_0_) | copy-start | bytes 64
  84.0 9.2 %collective-permute-start.14 = (f32[64,512]{1,0:T(8,128)}, f32[64,512]{1,0:T(8,128)S(1)}, u32[]{:S(2)}, u32[]{:S(2)}) collective-permute-start(f32[64,512]{1,0:T(8,128)} %get-tuple-element.43), channel_id=1, source_target_pairs={{0,1},{1,2},{2,3},{3,0},{4,5},{5,6},{6,7},{7,4},{8,9},{9,10},{10,1... | collective-permute-start | bytes 393224 | tf_op jit(solution)/shard_map/ppermute | solution.py:626
  84.4 8.8 %collective-permute-start.15 = (f32[64,512]{1,0:T(8,128)}, f32[64,512]{1,0:T(8,128)S(1)}, u32[]{:S(2)}, u32[]{:S(2)}) collective-permute-start(f32[64,512]{1,0:T(8,128)} %get-tuple-element.44), channel_id=1, source_target_pairs={{0,2},{1,3},{2,0},{3,1},{4,6},{5,7},{6,4},{7,5},{8,10},{9,11},{10,... | collective-permute-start | bytes 393224 | tf_op jit(solution)/shard_map/ppermute | solution.py:626
  85.8 7.7 %collective-permute-start.16 = (f32[64,512]{1,0:T(8,128)}, f32[64,512]{1,0:T(8,128)S(1)}, u32[]{:S(2)}, u32[]{:S(2)}) collective-permute-start(f32[64,512]{1,0:T(8,128)} %get-tuple-element.45), channel_id=1, source_target_pairs={{0,3},{1,0},{2,1},{3,2},{4,7},{5,4},{6,5},{7,6},{8,11},{9,8},{10,9... | collective-permute-start | bytes 393224 | tf_op jit(solution)/shard_map/ppermute | solution.py:626
  96.0 18.1 %all-to-all-start.3 = ((f32[32,8,128]{2,1,0:T(8,128)}), f32[32,8,128]{2,1,0:T(8,128)S(1)}, u32[]{:S(2)}, u32[]{:S(2)}) async-start(f32[32,8,128]{2,1,0:T(8,128)} %get-tuple-element.52), calls=%async_computation.3 | async-start | bytes 262144 | tf_op jit(solution)/shard_map/all_to_all | solution.py:639
  104.3 9.8 %collective-permute-start.18 = (f32[80,256]{1,0:T(8,128)S(1)}, f32[80,256]{1,0:T(8,128)S(1)}, u32[]{:S(2)}, u32[]{:S(2)}) collective-permute-start(f32[80,256]{1,0:T(8,128)S(1)} %get-tuple-element.54), channel_id=1, source_target_pairs={{3,0},{0,1},{7,4},{4,5},{11,8},{8,9},{15,12},{12,13},{19,16},{16,1... | collective-permute-start | bytes 245768 | tf_op jit(solution)/shard_map/ppermute | solution.py:533
  106.4 7.6 %collective-permute-start.19 = (f32[80,256]{1,0:T(8,128)S(1)}, f32[80,256]{1,0:T(8,128)S(1)}, u32[]{:S(2)}, u32[]{:S(2)}) collective-permute-start(f32[80,256]{1,0:T(8,128)S(1)} %get-tuple-element.55), channel_id=1, source_target_pairs={{2,0},{3,1},{6,4},{7,5},{10,8},{11,9},{14,12},{15,13},{18,16},{19,... | collective-permute-start | bytes 245768 | tf_op jit(solution)/shard_map/ppermute | solution.py:533
  107.7 6.3 %collective-permute-start.20 = (f32[80,256]{1,0:T(8,128)S(1)}, f32[80,256]{1,0:T(8,128)S(1)}, u32[]{:S(2)}, u32[]{:S(2)}) collective-permute-start(f32[80,256]{1,0:T(8,128)S(1)} %get-tuple-element.56), channel_id=1, source_target_pairs={{1,0},{2,1},{5,4},{6,5},{9,8},{10,9},{13,12},{14,13},{17,16},{18,1... | collective-permute-start | bytes 245768 | tf_op jit(solution)/shard_map/ppermute | solution.py:533
  109.0 5.1 %copy-start = (f32[32,1,8,8,1,256]{5,4,3,2,1,0:T(1,128)S(1)}, f32[32,1,8,8,1,256]{5,4,3,2,1,0:T(1,128)}, u32[]{:S(2)}) copy-start(f32[32,1,8,8,1,256]{5,4,3,2,1,0:T(1,128)} %param.3) | copy-start | bytes 6291460
  (5 other events, 4.6 us)
